TPU v7x, 128 devices: a whole 4x4x4 slice. The times are simulated.
128 devices in a mesh: cells: 16 (over y_hi, z, core), grow: 4 (over x), gcol: 2 (over y_lo).
Axes of the slice: x: 4, y: 4 (y_hi: 2, y_lo: 2; y = y_hi * 2 + y_lo), z: 4, core: 2. Of those that a mesh axis runs over, the one named last changes fastest.
Arguments:
- counts: int32 [18432, 4, 2, 1024], P('cells', 'grow', 'gcol'), may hold values from 0 to 2689, as said below
- gene_mean: float32 [4, 2, 1024], P('grow', 'gcol'), may hold values from 0.2 to 1.2
- gene_scale: float32 [4, 2, 1024], P('grow', 'gcol'), may hold values from 0.4 to 2
Outputs:
- coexpression: float32 [4, 2048, 2, 4, 1024], P('grow', 'cells', 'gcol')
Inputs may be any that keep to these rules, and one draw needn't show every extreme that they name: `counts`: every cell has at least one count.
All inputs are finite; a program needn't handle non-finite values.
Results may differ from a plain program's by a relative error of at most 0.0008.
Values may be sent and summed in bfloat16 or wider, within the bound.
No kernel may reach another device: no remote copies, remote signals or barrier semaphores. Data moves between devices by JAX's collectives and lax.ppermute only.
A program may use at most 384 MiB of HBM per device.

v0:
```python
import jax
import jax.numpy as jnp
from jax import lax
from jax.sharding import PartitionSpec as P

GENES = 8192


def per_device(counts, gene_mean, gene_scale):
    cell_rows = counts.shape[0]
    width = counts.shape[3]
    local = counts.reshape(cell_rows, width).astype(jnp.float32)
    partial_totals = jnp.sum(local, axis=1)
    totals = lax.psum(partial_totals, ("grow", "gcol"))
    lognorm = jnp.log1p(local * GENES / totals[:, None])
    standard = ((lognorm - gene_mean.reshape(1, width)) / gene_scale.reshape(1, width)).astype(
        jnp.bfloat16
    )
    n_grow = lax.axis_size("grow")
    n_gcol = lax.axis_size("gcol")
    row_values = lax.all_gather(standard.reshape(cell_rows, 1, width), "gcol", axis=1, tiled=True)
    col_values = lax.all_gather(standard.reshape(cell_rows, 1, width), "grow", axis=1, tiled=True)
    row_flat = row_values.reshape(cell_rows, n_gcol * width)
    col_flat = col_values.reshape(cell_rows, n_grow * width)
    panel_rows = row_flat.shape[1]
    n_cells = lax.axis_size("cells")
    owned = panel_rows // n_cells
    summed = lax.psum_scatter(
        lax.dot_general(
            row_flat, col_flat, (((0,), (0,)), ((), ())), preferred_element_type=jnp.float32
        ),
        "cells",
        scatter_dimension=0,
        tiled=True,
    )
    scaled = summed / (n_cells * cell_rows)
    return scaled.reshape(1, owned, 1, n_grow, width)


def solution(mesh):
    placed = (P("cells", "grow", "gcol", None), P("grow", "gcol", None), P("grow", "gcol", None))
    return jax.shard_map(
        per_device,
        mesh=mesh,
        in_specs=placed,
        out_specs=P("grow", "cells", "gcol", None, None),
        check_vma=False,
    )
```

profile of v0, /device:TPU:1, one launch (start us, length us, event | category | flops | bytes accessed | tf_op | source)
XLA Modules:
  0.0 494.5 jit_solution(14020196921608690569)
XLA Ops:
  6.5 0.0 copy-start
  6.5 0.0 copy-start.1
  6.5 0.0 all-gather.3.cloned.1.call-start
  6.5 3.1 fusion.4
  9.6 17.1 %psum.7 = f32[1152]{0:T(1024)S(1)} all-reduce(f32[1152]{0:T(1024)S(1)} %fusion.4), channel_id=1, replica_groups=mesh['cells'=16,'grow'=4,'gcol'=2] {'grow','gcol'}, use_global_device_ids=true, to_apply=%region_1.0 | all-reduce | flops 1152 | bytes 9216 | tf_op jit(solution)/shard_map/psum | solution.py:14
  26.7 0.0 copy-done
  26.7 0.0 copy-done.1
  26.7 5.6 %fusion.3 = bf16[1152,1,1024]{2,0,1:T(8,128)(2,1)} fusion(s32[1152,1,1,1024]{3,2,1,0:T(1,128)} %param.3, f32[1024]{0:T(1024)S(1)} %bitcast.19, f32[1024]{0:T(1024)S(1)} %bitcast.20, f32[1152]{0:T(1024)S(1)} %psum.7), kind=kLoop, calls=%fused_computation.5 | loop fusion | flops 7077888 | bytes 7090688 | tf_op jit(solution)/shard_map/convert_element_type | solution.py:16
  32.4 0.0 all-gather.3.cloned.1.call-update
  32.4 0.0 all-gather.5.cloned.1.call-start
  32.4 0.7 all-gather.5.cloned.1.call-update
  33.1 0.0 reduce-scatter.2.cloned.1.call-start
  33.2 67.8 %all-gather.3.cloned.1.call-done = bf16[1152,2,1024]{2,0,1:T(8,128)(2,1)} async-done(((bf16[1152,1,1024]{2,0,1:T(8,128)(2,1)}), bf16[1152,2,1024]{2,0,1:T(8,128)(2,1)}) %all-gather.3.cloned.1.call-update) | async-done | bytes 4718608 | tf_op jit(solution)/shard_map/all_gather | solution.py:21
  101.0 6.7 %copy.8 = bf16[1152,2,1024]{0,2,1:T(8,128)(2,1)} copy(bf16[1152,2,1024]{2,0,1:T(8,128)(2,1)} %all-gather.3.cloned.1.call-done) | data formatting | bytes 9437184 | tf_op jit(solution)/shard_map/all_gather | solution.py:21
  107.8 87.9 %all-gather.5.cloned.1.call-done = bf16[1152,4,1024]{2,0,1:T(8,128)(2,1)} async-done(((bf16[1152,1,1024]{2,0,1:T(8,128)(2,1)}), bf16[1152,4,1024]{2,0,1:T(8,128)(2,1)}) %all-gather.5.cloned.1.call-update) | async-done | bytes 9437200 | tf_op jit(solution)/shard_map/all_gather | solution.py:22
  195.7 12.6 %copy.9 = bf16[1152,4,1024]{0,2,1:T(8,128)(2,1)} copy(bf16[1152,4,1024]{2,0,1:T(8,128)(2,1)} %all-gather.5.cloned.1.call-done) | data formatting | bytes 18874368 | tf_op jit(solution)/shard_map/all_gather | solution.py:22
  208.3 29.0 %fusion.5 = f32[2048,4096]{1,0:T(8,128)} fusion(bf16[1152,2048]{0,1:T(8,128)(2,1)} %bitcast.18, bf16[1152,4096]{0,1:T(8,128)(2,1)} %bitcast.17), kind=kOutput, calls=%fused_computation.8 | convolution fusion | flops 19327352832 | bytes 47710208 | tf_op jit(solution)/shard_map/dot_general | solution.py:29
  237.3 0.0 reduce-scatter.2.cloned.1.call-update
  237.3 246.4 %reduce-scatter.2.cloned.1.call-done = f32[128,4096]{1,0:T(8,128)} async-done(((f32[2048,4096]{1,0:T(8,128)}), f32[128,4096]{1,0:T(8,128)}) %reduce-scatter.2.cloned.1.call-update) | async-done | bytes 2097168 | tf_op jit(solution)/shard_map/reduce_scatter | solution.py:28
  483.7 1.8 broadcast_multiply_fusion
  485.5 2.4 reshape.124
Async XLA Ops:
  6.5 20.2 %copy-start = (f32[1,1,1024]{2,1,0:T(1,128)S(1)}, f32[1,1,1024]{2,1,0:T(1,128)}, u32[]{:S(2)}) copy-start(f32[1,1,1024]{2,1,0:T(1,128)} %param.5) | copy-start | bytes 12292
  6.5 20.2 %copy-start.1 = (f32[1,1,1024]{2,1,0:T(1,128)S(1)}, f32[1,1,1024]{2,1,0:T(1,128)}, u32[]{:S(2)}) copy-start(f32[1,1,1024]{2,1,0:T(1,128)} %param.4) | copy-start | bytes 12292
  6.5 94.5 %all-gather.3.cloned.1.call-start = ((), (), s32[]{:S(2)}) async-start(), calls=%async_computation.1 | async-start | bytes 7077888 | tf_op jit(solution)/shard_map/all_gather | solution.py:21
  32.4 163.3 %all-gather.5.cloned.1.call-start = ((), (), s32[]{:S(2)}) async-start(), calls=%async_computation.2 | async-start | bytes 11796480 | tf_op jit(solution)/shard_map/all_gather | solution.py:22
  33.1 450.6 %reduce-scatter.2.cloned.1.call-start = ((), (), s32[]{:S(2)}) async-start(), calls=%async_computation.3 | async-start | bytes 35651584 | tf_op jit(solution)/shard_map/reduce_scatter | solution.py:28
Sparse Core Ops, SparseCore 0:
  32.5 68.4 all-gather.2
  102.7 92.9 all-gather.4
  237.4 246.2 reduce-scatter.1
where the time goes:
time: 497 us; the launch traced here: 494 us
  waiting for transfers between devices  403 us (81%)
  matrix products  29 us (6%)
  local copies, waits for them, and re-layouts  21.8 us (4%)
  blocking collectives  17.1 us (3%)
  between operations  13.1 us (3%)
  other arithmetic  10.4 us (2%)
    reduce_scatter x1, waiting for transfers between devices, per_device(): lax.psum_scatter(lax.dot_general(row_flat, col_flat, (((0,), (0,)), ((),...  246 us
    all_gather x1, waiting for transfers between devices, per_device(): lax.all_gather(standard.reshape(cell_rows, 1, width), 'grow', axis=1, til...  87.9 us
    all_gather x1, waiting for transfers between devices, per_device(): lax.all_gather(standard.reshape(cell_rows, 1, width), 'gcol', axis=1, til...  67.8 us
    dot_general x1, matrix products, per_device(): lax.dot_general(row_flat, col_flat, (((0,), (0,)), ((), ())), preferred_e...  29 us
    psum x1, blocking collectives, per_device(): totals = lax.psum(partial_totals, ('grow', 'gcol'))  17.1 us
    all_gather x1, local copies, waits for them, and re-layouts, per_device(): lax.all_gather(standard.reshape(cell_rows, 1, width), 'grow', axis=1, til...  12.6 us
  transfers between devices with their start and end apart: 3, of which 3 were waited for; matrix products, arithmetic and copies ran while one was open for 1% of the time, Pallas kernels for 0%

commit v1 on v0

v1 whole, which is shorter than its diff:
```python
import jax
import jax.numpy as jnp
import numpy as np
from jax import lax
from jax.experimental import pallas as pl
from jax.experimental.pallas import tpu as pltpu
from jax.sharding import PartitionSpec as P

GENES = 8192
CELLS = 18432
AXES = ("cells", "grow", "gcol")
SIZES = (2, 4, 2, 4, 2)
ROWS = 1152
DEPTH = 2 * ROWS
HALF = 512
ORDER = (0, 3, 2, 1)

ALPHA = 2.0**17 / 9.0e6
BETA = 32700.0 / float(np.log1p(2.0**17))
VMEM = 60 * 1024 * 1024


def moves(target):
    pairs = []
    for i, at in enumerate(np.ndindex(*SIZES)):
        to = tuple(v % s for v, s in zip(target(*at), SIZES))
        pairs.append((i, int(np.ravel_multi_index(to, SIZES))))
    return pairs


TO_CORE = moves(lambda h, z, c, x, b: (h, z, 1 - c, x, b))
TO_YLO = moves(lambda h, z, c, x, b: (h, z, c, x, 1 - b))
TO_YHI = moves(lambda h, z, c, x, b: (1 - h, z, c, x, b))
TO_YHI_CORE = moves(lambda h, z, c, x, b: (1 - h, z, 1 - c, x, b))
TO_X1 = moves(lambda h, z, c, x, b: (h, z, c, x ^ 1, b))
TO_X3 = moves(lambda h, z, c, x, b: (h, z, c, x ^ 3, b))
TO_Z1 = moves(lambda h, z, c, x, b: (h, z ^ 1, c, x, b))
TO_Z3 = moves(lambda h, z, c, x, b: (h, z ^ 3, c, x, b))
TO_SAME = moves(lambda h, z, c, x, b: (h, z, c, x - 1 + 2 * c, b))
TO_CROSS = moves(lambda h, z, c, x, b: (h, z, 1 - c, x + 1 - 2 * c, b))


def send(value, pairs):
    return lax.ppermute(value, AXES, pairs)


def encode(total):
    size = jnp.log(1.0 + ALPHA * jnp.abs(total)) * BETA + 0.5
    code = size.astype(jnp.int32)
    return jnp.where(total < 0, -code, code).astype(jnp.int16)


def decode(code):
    code = code.astype(jnp.int32).astype(jnp.float32)
    size = (jnp.exp(jnp.abs(code) * (1.0 / BETA)) - 1.0) * (1.0 / ALPHA)
    return jnp.where(code < 0, -size, size)


def params(flops=0, byte=0):
    return dict(
        compiler_params=pltpu.CompilerParams(vmem_limit_bytes=VMEM),
        cost_estimate=pl.CostEstimate(flops=flops, bytes_accessed=byte, transcendentals=0),
    )


def of(shape, dtype):
    return jax.ShapeDtypeStruct(shape, dtype)


def narrow(counts, core):
    steps = 8
    tile = ROWS // steps

    def body(core_ref, counts_ref, whole_ref, mine_ref, other_ref):
        whole_ref[...] = counts_ref[...].astype(jnp.int16)
        mine = core_ref[0]
        mine_ref[...] = counts_ref[:, pl.ds(pl.multiple_of(mine * HALF, HALF), HALF)].astype(jnp.int16)
        other_ref[...] = counts_ref[:, pl.ds(pl.multiple_of((1 - mine) * HALF, HALF), HALF)].astype(jnp.int16)

    return pl.pallas_call(
        body,
        out_shape=(of((ROWS, 1024), jnp.int16), of((ROWS, HALF), jnp.int16), of((ROWS, HALF), jnp.int16)),
        grid_spec=pltpu.PrefetchScalarGridSpec(
            num_scalar_prefetch=1,
            grid=(steps,),
            in_specs=[pl.BlockSpec((tile, 1024), lambda i, s: (i, 0))],
            out_specs=[
                pl.BlockSpec((tile, 1024), lambda i, s: (i, 0)),
                pl.BlockSpec((tile, HALF), lambda i, s: (i, 0)),
                pl.BlockSpec((tile, HALF), lambda i, s: (i, 0)),
            ],
        ),
        **params(byte=10 << 20),
    )(core, counts)


def standardized(count, factor, gene):
    value = count.astype(jnp.int32).astype(jnp.float32)
    return (jnp.log(1.0 + value * factor) * gene[0:1, :] - gene[1:2, :]).astype(jnp.bfloat16)


def row_groups(mine, sibling, factors, gene, z):
    order = jnp.array(ORDER, jnp.int32)
    lanes = jnp.concatenate([(order ^ z) * 2, (order ^ z) * 2 + 1])

    def body(lane_ref, mine_ref, sibling_ref, f_ref, g_ref, out_ref):
        gene_of = g_ref[...]
        out_ref[0, :, 0:ROWS] = standardized(mine_ref[...], f_ref[0:ROWS, :], gene_of).T
        out_ref[0, :, ROWS:DEPTH] = standardized(sibling_ref[...], f_ref[ROWS:DEPTH, :], gene_of).T

    return pl.pallas_call(
        body,
        out_shape=of((2, HALF, DEPTH), jnp.bfloat16),
        grid_spec=pltpu.PrefetchScalarGridSpec(
            num_scalar_prefetch=1,
            grid=(8,),
            in_specs=[
                pl.BlockSpec((ROWS, 128), lambda i, s: (0, s[i])),
                pl.BlockSpec((ROWS, 128), lambda i, s: (0, s[i])),
                pl.BlockSpec((DEPTH, 1), lambda i, s: (0, 0)),
                pl.BlockSpec((2, 128), lambda i, s: (0, s[i])),
            ],
            out_specs=pl.BlockSpec((1, 128, DEPTH), lambda i, s: (i // 4, i % 4, 0)),
        ),
        **params(byte=10 << 20),
    )(lanes, mine, sibling, factors, gene)


def column_chunks(pieces, factors):
    n = len(pieces)
    tiles = 4
    offsets = jnp.stack([jnp.asarray(p[3], jnp.int32) for p in pieces])

    def body(off_ref, *refs):
        out_ref = refs[-1]
        f_ref = refs[3 * n]
        i = pl.program_id(0)
        for k in range(n):

            @pl.when(i // tiles == k)
            def _():
                mine_ref, sibling_ref, g_ref = refs[3 * k : 3 * k + 3]
                gene_of = g_ref[...]
                out_ref[0, 0:ROWS, :] = standardized(mine_ref[...], f_ref[0:ROWS, :], gene_of)
                out_ref[0, ROWS:DEPTH, :] = standardized(sibling_ref[...], f_ref[ROWS:DEPTH, :], gene_of)

    def at(k):
        return lambda i, s: (0, s[k] * tiles + jnp.clip(i - k * tiles, 0, tiles - 1))

    in_specs, operands = [], []
    for k, (mine, sibling, gene, _) in enumerate(pieces):
        in_specs += [
            pl.BlockSpec((ROWS, 128), at(k)),
            pl.BlockSpec((ROWS, 128), at(k)),
            pl.BlockSpec((2, 128), at(k)),
        ]
        operands += [mine, sibling, gene]
    in_specs.append(pl.BlockSpec((DEPTH, 1), lambda i, s: (0, 0)))
    return pl.pallas_call(
        body,
        out_shape=of((n, DEPTH, HALF), jnp.bfloat16),
        grid_spec=pltpu.PrefetchScalarGridSpec(
            num_scalar_prefetch=1,
            grid=(n * tiles,),
            in_specs=in_specs,
            out_specs=pl.BlockSpec((1, DEPTH, 128), lambda i, s: (i // tiles, 0, i % tiles)),
        ),
        **params(byte=n * (5 << 20)),
    )(offsets, *operands, factors)


def products(steps, rows, cols):
    n = len(steps)
    combos = sorted({(r, c) for r, _, c, _ in steps})
    which = jnp.array([combos.index((r, c)) for r, _, c, _ in steps], jnp.int32)

    def last(array, place):
        table, now = [], next(s[place + 1] for s in steps if s[place] == array)
        for s in steps:
            now = s[place + 1] if s[place] == array else now
            table.append(now)
        return jnp.array(table, jnp.int32)

    tables = [last(r, 0) for r in range(len(rows))] + [last(c, 2) for c in range(len(cols))]

    def body(which_ref, *refs):
        refs = refs[len(tables) :]
        row_refs, col_refs = refs[: len(rows)], refs[len(rows) : len(rows) + len(cols)]
        send_a, send_b, keep_a, keep_b = refs[len(rows) + len(cols) :]
        for k, (r, c) in enumerate(combos):

            @pl.when(which_ref[pl.program_id(0)] == k)
            def _():
                left = row_refs[r][0]
                a = jnp.dot(left, col_refs[c][0, :, 0:256], preferred_element_type=jnp.float32)
                keep_a[0] = a[0:256].reshape(2, 128, 256)
                send_a[0] = encode(a[256:512]).reshape(2, 128, 256)
                b = jnp.dot(left, col_refs[c][0, :, 256:512], preferred_element_type=jnp.float32)
                keep_b[0, 0] = b[0:128]
                keep_b[0, 1] = b[384:512]
                send_b[0] = encode(b[128:384]).reshape(2, 128, 256)

    def row_map(k):
        return lambda i, which, *t: (t[k][i], 0, 0)

    in_specs = [pl.BlockSpec((1, HALF, DEPTH), row_map(k)) for k in range(len(rows))]
    in_specs += [pl.BlockSpec((1, DEPTH, HALF), row_map(len(rows) + k)) for k in range(len(cols))]
    out = pl.BlockSpec((1, 2, 128, 256), lambda i, *t: (i, 0, 0, 0))
    return pl.pallas_call(
        body,
        out_shape=(
            of((n, 2, 128, 256), jnp.int16),
            of((n, 2, 128, 256), jnp.int16),
            of((n, 2, 128, 256), jnp.float32),
            of((n, 2, 128, 256), jnp.float32),
        ),
        grid_spec=pltpu.PrefetchScalarGridSpec(
            num_scalar_prefetch=1 + len(tables), grid=(n,), in_specs=in_specs, out_specs=[out] * 4
        ),
        **params(flops=n * 2 * HALF * HALF * DEPTH, byte=n * (4 << 20)),
    )(which, *tables, *rows, *cols)


def second(keep_a, keep_b, got_a, got_b):
    n = keep_a.shape[0]

    def body(ka, kb, ga, gb, sa2, sb2, ka2, kb2):
        ka2[...] = ka[:, 0] + decode(ga[:, 1])
        sa2[...] = encode(ka[:, 1] + decode(ga[:, 0]))
        kb2[...] = kb[:, 0] + decode(gb[:, 0])
        sb2[...] = encode(kb[:, 1] + decode(gb[:, 1]))

    four = pl.BlockSpec((1, 2, 128, 256), lambda i: (i, 0, 0, 0))
    three = pl.BlockSpec((1, 128, 256), lambda i: (i, 0, 0))
    return pl.pallas_call(
        body,
        grid=(n,),
        out_shape=(
            of((n, 128, 256), jnp.int16),
            of((n, 128, 256), jnp.int16),
            of((n, 128, 256), jnp.float32),
            of((n, 128, 256), jnp.float32),
        ),
        in_specs=[four] * 4,
        out_specs=[three] * 4,
        **params(byte=n * (1 << 20)),
    )(keep_a, keep_b, got_a, got_b)


def summed_z(parts, groups, tables):
    chunks, rounds = len(tables), len(parts)
    used = np.array([[t[0] for t in row] for row in tables], np.int32)
    index = []
    for r in range(rounds):
        index.append(np.array([[t[1] if t[0] == r else 0 for t in row] for row in tables], np.int32))
    pick = jnp.stack([jnp.asarray(t)[:, groups].reshape(-1) for t in [used, *index]])

    def body(pick_ref, *refs):
        keep, to_c, to_y, to_yc = refs[4 * rounds :]
        i = pl.program_id(0)
        for r in range(rounds):

            @pl.when(pick_ref[0, i] == r)
            def _():
                ka, kb, ga, gb = refs[4 * r : 4 * r + 4]
                a, b = ka[0] + decode(ga[0]), kb[0] + decode(gb[0])

                @pl.when(i % 4 == 0)
                def _():
                    keep[0, :, 0:256] = a
                    keep[0, :, 256:512] = b

                for d, ref in ((1, to_c), (2, to_y), (3, to_yc)):

                    @pl.when(i % 4 == d)
                    def _():
                        ref[0, :, 0:256] = encode(a)
                        ref[0, :, 256:512] = encode(b)

    def at(r):
        return lambda i, s: (s[1 + r, i], 0, 0)

    in_specs = [pl.BlockSpec((1, 128, 256), at(r)) for r in range(rounds) for _ in range(4)]
    return pl.pallas_call(
        body,
        out_shape=(of((chunks, 128, HALF), jnp.float32),) + (of((chunks, 128, HALF), jnp.int16),) * 3,
        grid_spec=pltpu.PrefetchScalarGridSpec(
            num_scalar_prefetch=1,
            grid=(chunks * 4,),
            in_specs=in_specs,
            out_specs=[pl.BlockSpec((1, 128, HALF), lambda i, s: (i // 4, 0, 0))] * 4,
        ),
        **params(byte=chunks * (2 << 20)),
    )(pick, *[a for part in parts for a in part])


def finish(keep, got_c, got_y, got_yc, places, out=None):
    n = keep.shape[0]

    def body(place_ref, keep_ref, y_ref, c_ref, yc_ref, *rest):
        out_ref = rest[-1]
        i = pl.program_id(0)

        @pl.when(i < n)
        def _():
            out_ref[...] = (keep_ref[0] + decode(y_ref[0])) * (1.0 / CELLS)

        @pl.when(i >= n)
        def _():
            out_ref[...] = (decode(c_ref[0]) + decode(yc_ref[0])) * (1.0 / CELLS)

    mine = pl.BlockSpec((1, 128, HALF), lambda i, s: (jnp.minimum(i, n - 1), 0, 0))
    other = pl.BlockSpec((1, 128, HALF), lambda i, s: (jnp.maximum(i - n, 0), 0, 0))
    in_specs, operands, alias = [mine, mine, other, other], [keep, got_y, got_c, got_yc], {}
    if out is not None:
        in_specs.append(pl.BlockSpec(memory_space=pl.ANY))
        operands.append(out)
        alias = {5: 0}
    return pl.pallas_call(
        body,
        out_shape=of((128, 4096), jnp.float32),
        grid_spec=pltpu.PrefetchScalarGridSpec(
            num_scalar_prefetch=1,
            grid=(2 * n,),
            in_specs=in_specs,
            out_specs=pl.BlockSpec((128, HALF), lambda i, s: (0, s[i])),
        ),
        input_output_aliases=alias,
        **params(byte=n * (1 << 20)),
    )(places, *operands)


def per_device(counts, gene_mean, gene_scale):
    cells, x, b = lax.axis_index("cells"), lax.axis_index("grow"), lax.axis_index("gcol")
    high, z, core = cells // 8, (cells // 2) % 4, cells % 2
    counts = counts.reshape(ROWS, 1024)

    whole, first, other = narrow(counts, core.reshape(1))
    n0_mine, n0_sib = send(first, TO_SAME), send(other, TO_CROSS)
    y_mine = send(whole, TO_YLO)
    n1_mine, n1_sib = send(other, TO_SAME), send(first, TO_CROSS)
    whole_sib = send(whole, TO_CORE)

    inverse = 1.0 / gene_scale.reshape(1024)
    own = jnp.concatenate([inverse, gene_mean.reshape(1024) * inverse])
    total = jnp.sum(counts, axis=1).astype(jnp.float32)
    got = send(jnp.concatenate([total, own]), TO_YLO)
    total, gene_y = total + got[:ROWS], got[ROWS:]
    got = send(jnp.concatenate([total, own]), TO_X1)
    total, gene_1 = total + got[:ROWS], got[ROWS:]
    got = send(jnp.concatenate([total, own, gene_1]), TO_X3)
    total, gene_3, gene_2 = total + got[:ROWS], got[ROWS : ROWS + 2048], got[ROWS + 2048 :]
    factor = GENES / total
    factors = jnp.concatenate([factor, send(factor, TO_CORE)]).reshape(DEPTH, 1)
    gene_n = jnp.where((x + core) % 2 == 0, gene_1, gene_3).reshape(2, 1024)
    own, gene_y, gene_2 = own.reshape(2, 1024), gene_y.reshape(2, 1024), gene_2.reshape(2, 1024)

    own_rows = row_groups(whole, whole_sib, factors, own, z)
    flip = lambda v, h: jnp.where(h == 0, v, jnp.concatenate([v[:, HALF:], v[:, :HALF]], axis=1))
    gene_n = flip(gene_n, core)
    cols_1 = column_chunks([(whole, whole_sib, own, core), (n0_mine, n0_sib, gene_n, 0)], factors)
    sa, sb, ka, kb = products([(0, 0, 0, 0), (0, 1, 0, 0), (0, 0, 0, 1), (0, 1, 0, 1)], [own_rows], [cols_1])
    ga, gb = send(sa, TO_Z1), send(sb, TO_Z3)
    x2_mine, x2_sib = send(n0_mine, TO_SAME), send(n0_sib, TO_SAME)
    y_sib = send(y_mine, TO_CORE)
    sa, sb, ka, kb = second(ka, kb, ga, gb)
    round_1 = (ka, kb, send(sa, TO_Z3), send(sb, TO_Z1))

    y_rows = row_groups(y_mine, y_sib, factors, gene_y, z)
    cols_2 = column_chunks([(n1_mine, n1_sib, gene_n[:, HALF:], 0)], factors)
    steps = [(1, 0, 0, 0), (1, 1, 0, 0), (1, 0, 0, 1), (1, 1, 0, 1), (0, 0, 1, 0), (0, 1, 1, 0), (1, 0, 1, 0), (1, 1, 1, 0)]
    sa, sb, ka, kb = products(steps, [own_rows, y_rows], [cols_1, cols_2])
    ga, gb = send(sa, TO_Z1), send(sb, TO_Z3)
    sa, sb, ka, kb = second(ka, kb, ga, gb)
    round_2 = (ka, kb, send(sa, TO_Z3), send(sb, TO_Z1))

    cols_3 = column_chunks([(x2_mine, x2_sib, flip(gene_2, core), 0)], factors)
    steps = [(0, 0, 0, 0), (0, 1, 0, 0), (1, 0, 0, 0), (1, 1, 0, 0)]
    sa, sb, ka, kb = products(steps, [own_rows, y_rows], [cols_3])
    ga, gb = send(sa, TO_Z1), send(sb, TO_Z3)
    sa, sb, ka, kb = second(ka, kb, ga, gb)
    round_3 = (ka, kb, send(sa, TO_Z3), send(sb, TO_Z1))

    away = (b ^ high).astype(jnp.int32)
    groups = jnp.stack([2 * (dy ^ away) + (core ^ dc) for dy in (0, 1) for dc in (0, 1)])
    tables = [
        [(0, 0), (0, 1), (1, 0), (1, 1)],
        [(0, 2), (0, 3), (1, 2), (1, 3)],
        [(1, 4), (1, 5), (1, 6), (1, 7)],
    ]
    keep, to_c, to_y, to_yc = summed_z([round_1, round_2], groups, tables)
    near = (x + 1 - 2 * core) % 4
    far = (x - 1 + 2 * core) % 4
    opposite = x ^ 2
    places = jnp.stack(
        [2 * x + core, 2 * near + core, 2 * near + 1 - core, 2 * x + 1 - core, 2 * far + 1 - core, 2 * far + core]
    ).astype(jnp.int32)
    out = finish(keep, send(to_c, TO_CORE), send(to_y, TO_YHI), send(to_yc, TO_YHI_CORE), places)
    keep, to_c, to_y, to_yc = summed_z([round_3], groups, [[(0, 0), (0, 1), (0, 2), (0, 3)]])
    places = jnp.stack([2 * opposite + core, 2 * opposite + 1 - core]).astype(jnp.int32)
    out = finish(keep, send(to_c, TO_CORE), send(to_y, TO_YHI), send(to_yc, TO_YHI_CORE), places, out)
    return out.reshape(1, 128, 1, 4, 1024)


def solution(mesh):
    placed = (P("cells", "grow", "gcol", None), P("grow", "gcol", None), P("grow", "gcol", None))
    return jax.shard_map(
        per_device,
        mesh=mesh,
        in_specs=placed,
        out_specs=P("grow", "cells", "gcol", None, None),
        check_vma=False,
    )
```

time: 497 us -> 324 us (0.65)
  waiting for transfers between devices: 403 us -> 76.7 us
  Pallas kernels: 0 us -> 129 us
  starting transfers between devices: 0.08 us -> 54.1 us
  matrix products: 29 us -> 0 us
  other arithmetic: 10.4 us -> 29.5 us
  blocking collectives: 17.1 us -> 0 us
  between operations: 13.1 us -> 0.33 us
  local copies, waits for them, and re-layouts: 21.8 us -> 28.3 us
    reduce_scatter x1 -> x0, waiting for transfers between devices: 246 us -> none  [per_device(): lax.psum_scatter(lax.dot_general(row_flat, col_flat, (((0,), (0,)), ((),...]
    all_gather x2 -> x0, waiting for transfers between devices: 156 us -> none  [the longest x1 87.9 us: per_device(): lax.all_gather(standard.reshape(cell_rows, 1, width), 'grow', axis=1, til...]
    pallas_call x0 -> x16, Pallas kernels: none -> 129 us  [the longest x3 42.9 us: products(): pl.pallas_call(body, out_shape=(of((n, 2, 128, 256), jnp.int16), of((n, 2...]
    ppermute x0 -> x31, waiting for transfers between devices: none -> 76.7 us  [send(): return lax.ppermute(value, AXES, pairs)]
    ppermute x0 -> x31, starting transfers between devices: none -> 54.1 us  [send(): return lax.ppermute(value, AXES, pairs)]
    dot_general x1 -> x0, matrix products: 29 us -> none  [per_device(): lax.dot_general(row_flat, col_flat, (((0,), (0,)), ((), ())), preferred_e...]
    all_gather x2 -> x0, local copies, waits for them, and re-layouts: 19.4 us -> none  [the longest x1 12.6 us: per_device(): lax.all_gather(standard.reshape(cell_rows, 1, width), 'grow', axis=1, til...]
    reduce_sum x1, other arithmetic: 3.05 us -> 22.3 us  [per_device(): total = jnp.sum(counts, axis=1).astype(jnp.float32)]
  transfers between devices with their start and end apart: 3 -> 31, of which waited for: 3 -> 9; matrix products, arithmetic and copies ran while one was open for 1% -> 13% of each run, Pallas kernels for 0% -> 37%
where the time goes in v1:
time: 324 us; the launch traced here: 318 us
  Pallas kernels  129 us (40%)
  waiting for transfers between devices  76.7 us (24%)
  starting transfers between devices  54.1 us (17%)
  other arithmetic  29.5 us (9%)
  local copies, waits for them, and re-layouts  28.3 us (9%)
    ppermute x31, waiting for transfers between devices, send(): return lax.ppermute(value, AXES, pairs)  76.7 us
    ppermute x31, starting transfers between devices, send(): return lax.ppermute(value, AXES, pairs)  54.1 us
    pallas_call x3, Pallas kernels, products(): pl.pallas_call(body, out_shape=(of((n, 2, 128, 256), jnp.int16), of((n, 2...  42.9 us
    reduce_sum x1, other arithmetic, per_device(): total = jnp.sum(counts, axis=1).astype(jnp.float32)  22.3 us
    pallas_call x3, Pallas kernels, column_chunks(): pl.pallas_call(body, out_shape=of((n, DEPTH, HALF), jnp.bfloat16), grid_s...  19.9 us
    pallas_call x2, Pallas kernels, row_groups(): pl.pallas_call(body, out_shape=of((2, HALF, DEPTH), jnp.bfloat16), grid_s...  19.8 us
    pallas_call x3, Pallas kernels, second(): pl.pallas_call(body, grid=(n,), out_shape=(of((n, 128, 256), jnp.int16),...  15.9 us
    pallas_call x2, Pallas kernels, summed_z(): pl.pallas_call(body, out_shape=(of((chunks, 128, HALF), jnp.float32),) +...  14.7 us
  transfers between devices with their start and end apart: 31, of which 9 were waited for; matrix products, arithmetic and copies ran while one was open for 13% of the time, Pallas kernels for 37%

profile of v1, /device:TPU:1, one launch (start us, length us, event | category | flops | bytes accessed | tf_op | source)
XLA Modules:
  0.0 317.9 jit_solution(13730035243307437012)
XLA Ops:
  0.0 5.6 %copy.39 = s32[1152,1,1,1024]{3,0,1,2:T(8,128)} copy(s32[1152,1,1,1024]{3,2,1,0:T(1,128)} %param.22) | data formatting | bytes 9437184
  5.6 6.9 %shard_map.208 = (s16[1152,1024]{1,0:T(8,128)(2,1)}, s16[1152,512]{1,0:T(8,128)(2,1)}, s16[1152,512]{1,0:T(8,128)(2,1)}) custom-call(s32[1]{0:T(128)} %bitcast.9.core_ref, s32[1152,1024]{1,0:T(8,128)} %bitcast.26), custom_call_target="tpu_custom_call" | custom-call | bytes 10485760 | tf_op jit(solution)/shard_map/pallas_call | solution.py:80
  12.6 2.1 collective-permute-start.5
  14.7 1.0 collective-permute-start
  15.6 1.2 collective-permute-start.7
  16.9 22.3 %reduce_sum.9 = s32[1152]{0:T(1024)S(1)} reduce(s32[1152,1,1,1024]{3,2,1,0:T(1,128)} %param.22, s32[]{:T(128)} %constant.115.clone), dimensions={1,2,3}, to_apply=%region_0.1 | reduce | flops 1178496 | bytes 4723204 | tf_op jit(solution)/shard_map/reduce_sum | solution.py:346
  39.2 26.3 %collective-permute-done.5.mine_ref = s16[1152,1024]{1,0:T(8,128)(2,1)} collective-permute-done((s16[1152,1024]{1,0:T(8,128)(2,1)}, s16[1152,1024]{1,0:T(8,128)(2,1)}, u32[]{:S(2)}, u32[]{:S(2)}) %collective-permute-start.5) | collective-permute-done | bytes 2359328 | tf_op jit(solution)/shard_map/ppermute | solution.py:44
  65.6 1.6 collective-permute-start.6
  67.2 1.5 collective-permute-start.1
  68.7 1.1 collective-permute-done.1
  70.4 1.4 collective-permute-start.2
  71.8 1.2 collective-permute-done.2
  73.0 2.7 collective-permute-start.3
  75.8 2.6 collective-permute-start.9
  78.4 2.3 collective-permute-start.4
  81.2 1.3 reshape.197.g_ref.refs_2_
  82.7 3.2 %collective-permute-start.23 = (s16[1152,512]{1,0:T(8,128)(2,1)}, s16[1152,512]{1,0:T(8,128)(2,1)}, u32[]{:S(2)}, u32[]{:S(2)}) collective-permute-start(s16[1152,512]{1,0:T(8,128)(2,1)} %get-tuple-element.41), channel_id=1, source_target_pairs={{0,10},{1,11},{2,12},{3,13},{4,14},{5,15},{6,8},{7,9},{8,6},{9,7},... | collective-permute-start | bytes 3538952 | tf_op jit(solution)/shard_map/ppermute | solution.py:44
  87.9 0.7 slice.62
  89.2 1.4 slice_select_fusion
  90.6 0.7 select_n.80
  91.9 0.7 pad_maximum_fusion.5
  92.6 1.4 reshape.245.f_ref.refs_3_.refs_6_
  94.0 5.0 %collective-permute-done.9.refs_4_ = s16[1152,512]{1,0:T(8,128)(2,1)} collective-permute-done((s16[1152,512]{1,0:T(8,128)(2,1)}, s16[1152,512]{1,0:T(8,128)(2,1)}, u32[]{:S(2)}, u32[]{:S(2)}) %collective-permute-start.9) | collective-permute-done | bytes 1179680 | tf_op jit(solution)/shard_map/ppermute | solution.py:44
  99.1 3.7 %collective-permute-start.8 = (s16[1152,512]{1,0:T(8,128)(2,1)S(1)}, s16[1152,512]{1,0:T(8,128)(2,1)}, u32[]{:S(2)}, u32[]{:S(2)}) collective-permute-start(s16[1152,512]{1,0:T(8,128)(2,1)S(1)} %collective-permute-done.7.refs_3_), channel_id=1, source_target_pairs={{0,6},{1,7},{2,0},{3,1},{4,2},{5,3},{6,4},{7,5},{8,10},{9,11},{10,... | collective-permute-start | bytes 3538952 | tf_op jit(solution)/shard_map/ppermute | solution.py:44
  102.7 9.3 %collective-permute-done.22.refs_0_ = s16[1152,512]{1,0:T(8,128)(2,1)} collective-permute-done((s16[1152,512]{1,0:T(8,128)(2,1)}, s16[1152,512]{1,0:T(8,128)(2,1)}, u32[]{:S(2)}, u32[]{:S(2)}) %collective-permute-start.22) | collective-permute-done | bytes 1179680 | tf_op jit(solution)/shard_map/ppermute | solution.py:44
  112.0 12.3 %collective-permute-done.23.refs_1_ = s16[1152,512]{1,0:T(8,128)(2,1)} collective-permute-done((s16[1152,512]{1,0:T(8,128)(2,1)}, s16[1152,512]{1,0:T(8,128)(2,1)}, u32[]{:S(2)}, u32[]{:S(2)}) %collective-permute-start.23) | collective-permute-done | bytes 1179680 | tf_op jit(solution)/shard_map/ppermute | solution.py:44
  124.3 5.2 %shard_map.218.refs_7_ = bf16[1,2304,512]{2,1,0:T(8,128)(2,1)} custom-call(s32[1]{0:T(128)} %constant.113.clone.1.off_ref, s16[1152,512]{1,0:T(8,128)(2,1)} %collective-permute-done.22.refs_0_, s16[1152,512]{1,0:T(8,128)(2,1)} %collective-permute-done.23.refs_1_, f32[2,512]{1,0:T(2,128)} %slice.69.refs_2_, f32[2304,1]{1,0:T(8,128)} %reshape.245.f_ref.refs_3_.refs_6_), custom_call_target="tpu_custom_call" | custom-call | bytes 5242880 | tf_op jit(solution)/shard_map/pallas_call | solution.py:159
  129.6 1.5 copy-done.1
  131.0 9.9 %shard_map.209.refs_3_.refs_2_.refs_4_ = bf16[2,512,2304]{2,1,0:T(8,128)(2,1)} custom-call(s32[8]{0:T(128)} %pad_add_fusion.3.lane_ref, s16[1152,1024]{1,0:T(8,128)(2,1)} %get-tuple-element.40.mine_ref.refs_0_, s16[1152,1024]{1,0:T(8,128)(2,1)} %copy-done.1, f32[2304,1]{1,0:T(8,128)} %reshape.245.f_ref.refs_3_.refs_6_, f32[2,1024]{1,0:T(2,128)} %reshape.197.g_ref.refs_2_), custom_call_target="tpu_custom_call" | custom-call | bytes 10485760 | tf_op jit(solution)/shard_map/pallas_call | solution.py:111
  140.9 9.5 %shard_map.215.refs_3_.refs_6_ = bf16[2,2304,512]{2,1,0:T(8,128)(2,1)} custom-call(s32[2]{0:T(128)} %pad_add_fusion.4.off_ref, s16[1152,1024]{1,0:T(8,128)(2,1)} %get-tuple-element.40.mine_ref.refs_0_, s16[1152,1024]{1,0:T(8,128)(2,1)} %copy-done.1, f32[2,1024]{1,0:T(2,128)} %reshape.197.g_ref.refs_2_, s16[1152,512]{1,0:T(8,128)(2,1)} %copy-done.2, ...), custom_call_target="tpu_custom_call" | custom-call | bytes 10485760 | tf_op jit(solution)/shard_map/pallas_call | solution.py:159
  150.5 9.8 %shard_map.210.refs_4_.refs_5_ = bf16[2,512,2304]{2,1,0:T(8,128)(2,1)} custom-call(s32[8]{0:T(128)} %pad_add_fusion.3.lane_ref, s16[1152,1024]{1,0:T(8,128)(2,1)} %collective-permute-done.5.mine_ref, s16[1152,1024]{1,0:T(8,128)(2,1)} %collective-permute-done.6.sibling_ref, f32[2304,1]{1,0:T(8,128)} %reshape.245.f_ref.refs_3_.refs_6_, f32[2,1024]{1,0:T(2,128)} %reshape.198.g_ref), custom_call_target="tpu_custom_call" | custom-call | bytes 10485760 | tf_op jit(solution)/shard_map/pallas_call | solution.py:111
  160.8 19.9 %shard_map.219 = (s16[8,2,128,256]{3,2,1,0:T(8,128)(2,1)}, s16[8,2,128,256]{3,2,1,0:T(8,128)(2,1)}, f32[8,2,128,256]{3,2,1,0:T(8,128)}, f32[8,2,128,256]{3,2,1,0:T(8,128)}) custom-call(s32[8]{0:T(128)} %constant.118.clone.which_ref, s32[8]{0:T(128)} %constant.119.clone.refs_0_, s32[8]{0:T(128)} %constant.120.clone.refs_1_, s32[8]{0:T(128)} %constant.121.clone.refs_2_, ...), custom_call_target="tpu_custom_call" | custom-call | flops 9663676416 | bytes 33554432 | tf_op jit(solution)/shard_map/pallas_call | solution.py:209
  180.7 1.7 collective-permute-start.24
  182.4 2.2 collective-permute-start.25
  185.1 11.6 %shard_map.216 = (s16[4,2,128,256]{3,2,1,0:T(8,128)(2,1)}, s16[4,2,128,256]{3,2,1,0:T(8,128)(2,1)}, f32[4,2,128,256]{3,2,1,0:T(8,128)}, f32[4,2,128,256]{3,2,1,0:T(8,128)}) custom-call(s32[4]{0:T(128)} %broadcast.48.refs_2_.which_ref, s32[4]{0:T(128)} %constant.116.clone.refs_0_, s32[4]{0:T(128)} %constant.117.clone.which_ref.refs_1_, ...), custom_call_target="tpu_custom_call" | custom-call | flops 4831838208 | bytes 16777216 | tf_op jit(solution)/shard_map/pallas_call | solution.py:209
  196.7 0.7 collective-permute-start.18
  198.7 5.2 %shard_map.211.refs_5_ = bf16[1,2304,512]{2,1,0:T(8,128)(2,1)} custom-call(s32[1]{0:T(128)} %constant.113.clone.1.off_ref, s16[1152,512]{1,0:T(8,128)(2,1)} %collective-permute-done.8.refs_0_, s16[1152,512]{1,0:T(8,128)(2,1)} %collective-permute-done.10.refs_1_, f32[2,1024]{1,0:T(2,128)} %maximum_select_fusion.refs_2_, f32[2304,1]{1,0:T(8,128)} %reshape.245.f_ref.refs_3_.refs_6_), custom_call_target="tpu_custom_call" | custom-call | bytes 5242880 | tf_op jit(solution)/shard_map/pallas_call | solution.py:159
  203.9 10.8 %collective-permute-done.18.ga = s16[4,2,128,256]{3,2,1,0:T(8,128)(2,1)} collective-permute-done((s16[4,2,128,256]{3,2,1,0:T(8,128)(2,1)}, s16[4,2,128,256]{3,2,1,0:T(8,128)(2,1)}, u32[]{:S(2)}, u32[]{:S(2)}) %collective-permute-start.18) | collective-permute-done | bytes 524320 | tf_op jit(solution)/shard_map/ppermute | solution.py:44
  214.7 2.3 collective-permute-done.19.gb
  217.0 0.8 copy-done.9
  217.8 4.2 %shard_map.217 = (s16[4,128,256]{2,1,0:T(8,128)(2,1)}, s16[4,128,256]{2,1,0:T(8,128)(2,1)}, f32[4,128,256]{2,1,0:T(8,128)}, f32[4,128,256]{2,1,0:T(8,128)}) custom-call(f32[4,2,128,256]{3,2,1,0:T(8,128)} %get-tuple-element.55.ka, f32[4,2,128,256]{3,2,1,0:T(8,128)} %get-tuple-element.56.kb, s16[4,2,128,256]{3,2,1,0:T(8,128)(2,1)} %collective-permute-done.18.ga, ...), custom_call_target="tpu_custom_call" | custom-call | bytes 4194304 | tf_op jit(solution)/shard_map/pallas_call | solution.py:235
  222.0 2.3 collective-permute-start.20
  224.3 1.0 copy-done.3
  225.6 7.4 %shard_map.220 = (s16[8,128,256]{2,1,0:T(8,128)(2,1)}, s16[8,128,256]{2,1,0:T(8,128)(2,1)}, f32[8,128,256]{2,1,0:T(8,128)}, f32[8,128,256]{2,1,0:T(8,128)}) custom-call(f32[8,2,128,256]{3,2,1,0:T(8,128)} %get-tuple-element.63.ka, f32[8,2,128,256]{3,2,1,0:T(8,128)} %get-tuple-element.64.kb, s16[8,2,128,256]{3,2,1,0:T(8,128)(2,1)} %copy-done.3, ...), custom_call_target="tpu_custom_call" | custom-call | bytes 8388608 | tf_op jit(solution)/shard_map/pallas_call | solution.py:235
  233.6 11.4 %shard_map.212 = (s16[4,2,128,256]{3,2,1,0:T(8,128)(2,1)}, s16[4,2,128,256]{3,2,1,0:T(8,128)(2,1)}, f32[4,2,128,256]{3,2,1,0:T(8,128)}, f32[4,2,128,256]{3,2,1,0:T(8,128)}) custom-call(s32[4]{0:T(128)} %constant.117.clone.which_ref.refs_1_, s32[4]{0:T(128)} %constant.122.clone.refs_0_, s32[4]{0:T(128)} %constant.123.clone.refs_1_, ...), custom_call_target="tpu_custom_call" | custom-call | flops 4831838208 | bytes 16777216 | tf_op jit(solution)/shard_map/pallas_call | solution.py:209
  245.0 1.3 collective-permute-start.11
  246.3 2.2 collective-permute-start.12
  251.8 8.2 %collective-permute-done.21.refs_3_ = s16[4,128,256]{2,1,0:T(8,128)(2,1)S(1)} collective-permute-done((s16[4,128,256]{2,1,0:T(8,128)(2,1)S(1)}, s16[4,128,256]{2,1,0:T(8,128)(2,1)S(1)}, u32[]{:S(2)}, u32[]{:S(2)}) %collective-permute-start.21) | collective-permute-done | bytes 262176 | tf_op jit(solution)/shard_map/ppermute | solution.py:44
  261.1 10.4 %shard_map.221 = (f32[3,128,512]{2,1,0:T(8,128)}, s16[3,128,512]{2,1,0:T(8,128)(2,1)}, s16[3,128,512]{2,1,0:T(8,128)(2,1)}, s16[3,128,512]{2,1,0:T(8,128)(2,1)}) custom-call(s32[3,12]{1,0:T(4,128)} %pad_add_fusion.pick_ref, f32[4,128,256]{2,1,0:T(8,128)} %get-tuple-element.59.refs_0_, f32[4,128,256]{2,1,0:T(8,128)} %get-tuple-element.60.refs_1_, ...), custom_call_target="tpu_custom_call" | custom-call | bytes 6291456 | tf_op jit(solution)/shard_map/pallas_call | solution.py:284
  271.5 3.0 collective-permute-start.28
  274.5 0.8 copy-done.7
  275.5 4.2 %shard_map.213 = (s16[4,128,256]{2,1,0:T(8,128)(2,1)}, s16[4,128,256]{2,1,0:T(8,128)(2,1)}, f32[4,128,256]{2,1,0:T(8,128)}, f32[4,128,256]{2,1,0:T(8,128)}) custom-call(f32[4,2,128,256]{3,2,1,0:T(8,128)} %get-tuple-element.43.ka, f32[4,2,128,256]{3,2,1,0:T(8,128)} %get-tuple-element.44.kb, s16[4,2,128,256]{3,2,1,0:T(8,128)(2,1)} %copy-done.7, ...), custom_call_target="tpu_custom_call" | custom-call | bytes 4194304 | tf_op jit(solution)/shard_map/pallas_call | solution.py:235
  279.7 2.3 collective-permute-start.13
  282.4 6.2 %collective-permute-start.29 = (s16[3,128,512]{2,1,0:T(8,128)(2,1)S(1)}, s16[3,128,512]{2,1,0:T(8,128)(2,1)S(1)}, u32[]{:S(2)}, u32[]{:S(2)}) collective-permute-start(s16[3,128,512]{2,1,0:T(8,128)(2,1)S(1)} %copy-done.31), channel_id=1, source_target_pairs={{0,8},{1,9},{2,10},{3,11},{4,12},{5,13},{6,14},{7,15},{8,0},{9,1},... | collective-permute-start | bytes 1179656 | tf_op jit(solution)/shard_map/ppermute | solution.py:44
  290.6 0.7 copy-done.15
  291.4 4.4 %shard_map.214 = (f32[1,128,512]{2,1,0:T(8,128)}, s16[1,128,512]{2,1,0:T(8,128)(2,1)}, s16[1,128,512]{2,1,0:T(8,128)(2,1)}, s16[1,128,512]{2,1,0:T(8,128)(2,1)}) custom-call(s32[2,4]{1,0:T(2,128)} %pad_add_fusion.1.pick_ref, f32[4,128,256]{2,1,0:T(8,128)} %get-tuple-element.47.refs_0_, f32[4,128,256]{2,1,0:T(8,128)} %get-tuple-element.48.refs_1_, ...), custom_call_target="tpu_custom_call" | custom-call | bytes 2097152 | tf_op jit(solution)/shard_map/pallas_call | solution.py:284
  295.8 2.9 collective-permute-start.15
  298.7 1.1 collective-permute-start.16
  299.7 2.9 collective-permute-start.17
  302.6 0.7 stack.70.place_ref
  303.8 0.7 copy-done.11
  304.7 5.9 %shard_map.222.rest_0_ = f32[128,4096]{1,0:T(8,128)} custom-call(s32[6]{0:T(128)} %stack.70.place_ref, f32[3,128,512]{2,1,0:T(8,128)} %get-tuple-element.71.keep_ref, s16[3,128,512]{2,1,0:T(8,128)(2,1)} %copy-done.10, s16[3,128,512]{2,1,0:T(8,128)(2,1)} %copy-done.11, s16[3,128,512]{2,1,0:T(8,128)(2,1)} %copy-done.12), custom_call_target="tpu_custom_call" | custom-call | bytes 3145728 | tf_op jit(solution)/shard_map/pallas_call | solution.py:319
  311.4 2.9 shard_map.223
  314.3 3.6 %reshape.200 = f32[1,128,1,4,1024]{4,3,1,2,0:T(4,128)} reshape(f32[128,4096]{1,0:T(8,128)} %shard_map.223) | data formatting | bytes 4194304 | tf_op jit(solution)/shard_map/reshape | solution.py:402
  (130 shorter events, 16.0 us)
Async XLA Ops:
  5.6 11.2 %copy-start.29 = (f32[1,1,1024]{2,1,0:T(1,128)S(1)}, f32[1,1,1024]{2,1,0:T(1,128)}, u32[]{:S(2)}) copy-start(f32[1,1,1024]{2,1,0:T(1,128)} %param.24) | copy-start | bytes 12292
  12.6 53.0 %collective-permute-start.5 = (s16[1152,1024]{1,0:T(8,128)(2,1)}, s16[1152,1024]{1,0:T(8,128)(2,1)}, u32[]{:S(2)}, u32[]{:S(2)}) collective-permute-start(s16[1152,1024]{1,0:T(8,128)(2,1)} %get-tuple-element.40.mine_ref.refs_0_), channel_id=1, source_target_pairs={{0,1},{1,0},{2,3},{3,2},{4,5},{5,4},{6,7},{7,6},{8,9},{9,8},{10,11... | collective-permute-start | bytes 7077896 | tf_op jit(solution)/shard_map/ppermute | solution.py:44
  14.7 114.9 %collective-permute-start = (s16[1152,1024]{1,0:T(8,128)(2,1)}, s16[1152,1024]{1,0:T(8,128)(2,1)S(1)}, u32[]{:S(2)}, u32[]{:S(2)}) collective-permute-start(s16[1152,1024]{1,0:T(8,128)(2,1)} %get-tuple-element.40.mine_ref.refs_0_), channel_id=1, source_target_pairs={{0,8},{1,9},{2,10},{3,11},{4,12},{5,13},{6,14},{7,15},{8,0},{9,1},... | collective-permute-start | bytes 7077896 | tf_op jit(solution)/shard_map/ppermute | solution.py:44
  15.6 67.0 %collective-permute-start.7 = (s16[1152,512]{1,0:T(8,128)(2,1)}, s16[1152,512]{1,0:T(8,128)(2,1)S(1)}, u32[]{:S(2)}, u32[]{:S(2)}) collective-permute-start(s16[1152,512]{1,0:T(8,128)(2,1)} %get-tuple-element.41), channel_id=1, source_target_pairs={{0,6},{1,7},{2,0},{3,1},{4,2},{5,3},{6,4},{7,5},{8,10},{9,11},{10,... | collective-permute-start | bytes 3538952 | tf_op jit(solution)/shard_map/ppermute | solution.py:44
  16.9 22.3 %copy-start.28 = (f32[1,1,1024]{2,1,0:T(1,128)S(1)}, f32[1,1,1024]{2,1,0:T(1,128)}, u32[]{:S(2)}) copy-start(f32[1,1,1024]{2,1,0:T(1,128)} %param.23) | copy-start | bytes 12292
  65.6 84.9 %collective-permute-start.6 = (s16[1152,1024]{1,0:T(8,128)(2,1)}, s16[1152,1024]{1,0:T(8,128)(2,1)}, u32[]{:S(2)}, u32[]{:S(2)}) collective-permute-start(s16[1152,1024]{1,0:T(8,128)(2,1)} %collective-permute-done.5.mine_ref), channel_id=1, source_target_pairs={{0,8},{1,9},{2,10},{3,11},{4,12},{5,13},{6,14},{7,15},{8,0},{9,1},... | collective-permute-start | bytes 7077896 | tf_op jit(solution)/shard_map/ppermute | solution.py:44
  67.2 2.6 collective-permute-start.1
  69.8 0.6 copy-start.27
  70.4 2.6 collective-permute-start.2
  73.0 5.3 %copy-start.24 = (f32[3200]{0:T(1024)}, f32[3200]{0:T(1024)S(1)}, u32[]{:S(2)}) copy-start(f32[3200]{0:T(1024)S(1)} %collective-permute-done.2) | copy-start | bytes 38404
  73.0 5.3 %collective-permute-start.3 = (f32[5248]{0:T(1024)S(1)}, f32[5248]{0:T(1024)S(1)}, u32[]{:S(2)}, u32[]{:S(2)}) collective-permute-start(f32[5248]{0:T(1024)S(1)} %pad_maximum_fusion), channel_id=1, source_target_pairs={{0,6},{1,7},{2,4},{3,5},{4,2},{5,3},{6,0},{7,1},{8,14},{9,15},{10,... | collective-permute-start | bytes 62984 | tf_op jit(solution)/shard_map/ppermute | solution.py:44
  75.8 23.3 %collective-permute-start.9 = (s16[1152,512]{1,0:T(8,128)(2,1)}, s16[1152,512]{1,0:T(8,128)(2,1)}, u32[]{:S(2)}, u32[]{:S(2)}) collective-permute-start(s16[1152,512]{1,0:T(8,128)(2,1)} %get-tuple-element.42), channel_id=1, source_target_pairs={{0,10},{1,11},{2,12},{3,13},{4,14},{5,15},{6,8},{7,9},{8,6},{9,7},... | collective-permute-start | bytes 3538952 | tf_op jit(solution)/shard_map/ppermute | solution.py:44
  78.3 2.3 copy-start.26
  78.4 4.2 %collective-permute-start.4 = (f32[1152]{0:T(1024)S(1)}, f32[1152]{0:T(1024)}, u32[]{:S(2)}, u32[]{:S(2)}) collective-permute-start(f32[1152]{0:T(1024)S(1)} %fusion), channel_id=1, source_target_pairs={{0,8},{1,9},{2,10},{3,11},{4,12},{5,13},{6,14},{7,15},{8,0},{9,1},... | collective-permute-start | bytes 13832 | tf_op jit(solution)/shard_map/ppermute | solution.py:44
  82.5 29.5 %collective-permute-start.22 = (s16[1152,512]{1,0:T(8,128)(2,1)}, s16[1152,512]{1,0:T(8,128)(2,1)}, u32[]{:S(2)}, u32[]{:S(2)}) collective-permute-start(s16[1152,512]{1,0:T(8,128)(2,1)} %get-tuple-element.42), channel_id=1, source_target_pairs={{0,6},{1,7},{2,0},{3,1},{4,2},{5,3},{6,4},{7,5},{8,10},{9,11},{10,... | collective-permute-start | bytes 3538952 | tf_op jit(solution)/shard_map/ppermute | solution.py:44
  82.7 46.9 %copy-start.2 = (s16[1152,512]{1,0:T(8,128)(2,1)}, s16[1152,512]{1,0:T(8,128)(2,1)S(1)}, u32[]{:S(2)}) copy-start(s16[1152,512]{1,0:T(8,128)(2,1)S(1)} %collective-permute-done.7.refs_3_) | copy-start | bytes 3538948
  82.7 41.7 %collective-permute-start.23 = (s16[1152,512]{1,0:T(8,128)(2,1)}, s16[1152,512]{1,0:T(8,128)(2,1)}, u32[]{:S(2)}, u32[]{:S(2)}) collective-permute-start(s16[1152,512]{1,0:T(8,128)(2,1)} %get-tuple-element.41), channel_id=1, source_target_pairs={{0,10},{1,11},{2,12},{3,13},{4,14},{5,15},{6,8},{7,9},{8,6},{9,7},... | collective-permute-start | bytes 3538952 | tf_op jit(solution)/shard_map/ppermute | solution.py:44
  91.3 38.2 %copy-start.23 = (f32[2,1024]{1,0:T(2,128)}, f32[2,1024]{1,0:T(2,128)S(1)}, u32[]{:S(2)}) copy-start(f32[2,1024]{1,0:T(2,128)S(1)} %maximum_select_fusion.1.refs_5_) | copy-start | bytes 24580
  99.1 98.4 %collective-permute-start.8 = (s16[1152,512]{1,0:T(8,128)(2,1)S(1)}, s16[1152,512]{1,0:T(8,128)(2,1)}, u32[]{:S(2)}, u32[]{:S(2)}) collective-permute-start(s16[1152,512]{1,0:T(8,128)(2,1)S(1)} %collective-permute-done.7.refs_3_), channel_id=1, source_target_pairs={{0,6},{1,7},{2,0},{3,1},{4,2},{5,3},{6,4},{7,5},{8,10},{9,11},{10,... | collective-permute-start | bytes 3538952 | tf_op jit(solution)/shard_map/ppermute | solution.py:44
  112.0 86.7 %collective-permute-start.10 = (s16[1152,512]{1,0:T(8,128)(2,1)}, s16[1152,512]{1,0:T(8,128)(2,1)}, u32[]{:S(2)}, u32[]{:S(2)}) collective-permute-start(s16[1152,512]{1,0:T(8,128)(2,1)} %collective-permute-done.9.refs_4_), channel_id=1, source_target_pairs={{0,6},{1,7},{2,0},{3,1},{4,2},{5,3},{6,4},{7,5},{8,10},{9,11},{10,... | collective-permute-start | bytes 3538952 | tf_op jit(solution)/shard_map/ppermute | solution.py:44
  129.6 1.5 copy-start.1
  180.7 43.6 %collective-permute-start.24 = (s16[8,2,128,256]{3,2,1,0:T(8,128)(2,1)}, s16[8,2,128,256]{3,2,1,0:T(8,128)(2,1)S(1)}, u32[]{:S(2)}, u32[]{:S(2)}) collective-permute-start(s16[8,2,128,256]{3,2,1,0:T(8,128)(2,1)} %get-tuple-element.65), channel_id=1, source_target_pairs={{0,16},{1,17},{2,18},{3,19},{4,20},{5,21},{6,22},{7,23},{8,24},{9,... | collective-permute-start | bytes 3145736 | tf_op jit(solution)/shard_map/ppermute | solution.py:44
  182.4 41.9 %collective-permute-start.25 = (s16[8,2,128,256]{3,2,1,0:T(8,128)(2,1)}, s16[8,2,128,256]{3,2,1,0:T(8,128)(2,1)S(1)}, u32[]{:S(2)}, u32[]{:S(2)}) collective-permute-start(s16[8,2,128,256]{3,2,1,0:T(8,128)(2,1)} %get-tuple-element.66), channel_id=1, source_target_pairs={{0,48},{1,49},{2,50},{3,51},{4,52},{5,53},{6,54},{7,55},{8,56},{9,... | collective-permute-start | bytes 3145736 | tf_op jit(solution)/shard_map/ppermute | solution.py:44
  185.1 13.0 %copy-start.25 = (f32[2048]{0:T(1024)S(1)}, f32[2048]{0:T(1024)}, u32[]{:S(2)}) copy-start(f32[2048]{0:T(1024)} %get-tuple-element.76) | copy-start | bytes 24580
  196.7 18.0 %collective-permute-start.18 = (s16[4,2,128,256]{3,2,1,0:T(8,128)(2,1)}, s16[4,2,128,256]{3,2,1,0:T(8,128)(2,1)}, u32[]{:S(2)}, u32[]{:S(2)}) collective-permute-start(s16[4,2,128,256]{3,2,1,0:T(8,128)(2,1)} %get-tuple-element.57), channel_id=1, source_target_pairs={{0,16},{1,17},{2,18},{3,19},{4,20},{5,21},{6,22},{7,23},{8,24},{9,... | collective-permute-start | bytes 1572872 | tf_op jit(solution)/shard_map/ppermute | solution.py:44
  197.5 19.5 %collective-permute-start.19 = (s16[4,2,128,256]{3,2,1,0:T(8,128)(2,1)}, s16[4,2,128,256]{3,2,1,0:T(8,128)(2,1)S(1)}, u32[]{:S(2)}, u32[]{:S(2)}) collective-permute-start(s16[4,2,128,256]{3,2,1,0:T(8,128)(2,1)} %get-tuple-element.58), channel_id=1, source_target_pairs={{0,48},{1,49},{2,50},{3,51},{4,52},{5,53},{6,54},{7,55},{8,56},{9,... | collective-permute-start | bytes 1572872 | tf_op jit(solution)/shard_map/ppermute | solution.py:44
  217.0 0.8 copy-start.9
  222.0 26.5 %collective-permute-start.20 = (s16[4,128,256]{2,1,0:T(8,128)(2,1)}, s16[4,128,256]{2,1,0:T(8,128)(2,1)S(1)}, u32[]{:S(2)}, u32[]{:S(2)}) collective-permute-start(s16[4,128,256]{2,1,0:T(8,128)(2,1)} %get-tuple-element.61), channel_id=1, source_target_pairs={{0,48},{1,49},{2,50},{3,51},{4,52},{5,53},{6,54},{7,55},{8,56},{9,... | collective-permute-start | bytes 786440 | tf_op jit(solution)/shard_map/ppermute | solution.py:44
  224.3 1.0 copy-start.3
  224.3 1.3 copy-start.4
  233.0 27.0 %collective-permute-start.26 = (s16[8,128,256]{2,1,0:T(8,128)(2,1)}, s16[8,128,256]{2,1,0:T(8,128)(2,1)S(1)}, u32[]{:S(2)}, u32[]{:S(2)}) collective-permute-start(s16[8,128,256]{2,1,0:T(8,128)(2,1)} %get-tuple-element.69), channel_id=1, source_target_pairs={{0,48},{1,49},{2,50},{3,51},{4,52},{5,53},{6,54},{7,55},{8,56},{9,... | collective-permute-start | bytes 1572872 | tf_op jit(solution)/shard_map/ppermute | solution.py:44
  233.5 15.1 %copy-start.32 = (s16[4,128,256]{2,1,0:T(8,128)(2,1)S(1)}, s16[4,128,256]{2,1,0:T(8,128)(2,1)}, u32[]{:S(2)}) copy-start(s16[4,128,256]{2,1,0:T(8,128)(2,1)} %get-tuple-element.62) | copy-start | bytes 786436
  233.5 15.5 %copy-start.22 = (s32[3,4]{0,1:T(4,128)S(1)}, s32[3,4]{0,1:T(4,128)}, u32[]{:S(2)}) copy-start(s32[3,4]{0,1:T(4,128)} %constant.126.clone) | copy-start | bytes 148
  233.5 16.2 %copy-start.21 = (s32[3,4]{0,1:T(4,128)S(1)}, s32[3,4]{0,1:T(4,128)}, u32[]{:S(2)}) copy-start(s32[3,4]{0,1:T(4,128)} %constant.125.clone) | copy-start | bytes 148
  233.5 17.0 %copy-start.20 = (s32[3,4]{0,1:T(4,128)S(1)}, s32[3,4]{0,1:T(4,128)}, u32[]{:S(2)}) copy-start(s32[3,4]{0,1:T(4,128)} %constant.124.clone) | copy-start | bytes 148
  233.5 26.5 %collective-permute-start.27 = (s16[8,128,256]{2,1,0:T(8,128)(2,1)}, s16[8,128,256]{2,1,0:T(8,128)(2,1)S(1)}, u32[]{:S(2)}, u32[]{:S(2)}) collective-permute-start(s16[8,128,256]{2,1,0:T(8,128)(2,1)} %get-tuple-element.70), channel_id=1, source_target_pairs={{0,16},{1,17},{2,18},{3,19},{4,20},{5,21},{6,22},{7,23},{8,24},{9,... | collective-permute-start | bytes 1572872 | tf_op jit(solution)/shard_map/ppermute | solution.py:44
  245.0 29.5 %collective-permute-start.11 = (s16[4,2,128,256]{3,2,1,0:T(8,128)(2,1)}, s16[4,2,128,256]{3,2,1,0:T(8,128)(2,1)S(1)}, u32[]{:S(2)}, u32[]{:S(2)}) collective-permute-start(s16[4,2,128,256]{3,2,1,0:T(8,128)(2,1)} %get-tuple-element.45), channel_id=1, source_target_pairs={{0,16},{1,17},{2,18},{3,19},{4,20},{5,21},{6,22},{7,23},{8,24},{9,... | collective-permute-start | bytes 1572872 | tf_op jit(solution)/shard_map/ppermute | solution.py:44
  246.3 28.2 %collective-permute-start.12 = (s16[4,2,128,256]{3,2,1,0:T(8,128)(2,1)}, s16[4,2,128,256]{3,2,1,0:T(8,128)(2,1)S(1)}, u32[]{:S(2)}, u32[]{:S(2)}) collective-permute-start(s16[4,2,128,256]{3,2,1,0:T(8,128)(2,1)} %get-tuple-element.46), channel_id=1, source_target_pairs={{0,48},{1,49},{2,50},{3,51},{4,52},{5,53},{6,54},{7,55},{8,56},{9,... | collective-permute-start | bytes 1572872 | tf_op jit(solution)/shard_map/ppermute | solution.py:44
  248.6 11.5 %copy-start.13 = (s16[4,128,256]{2,1,0:T(8,128)(2,1)}, s16[4,128,256]{2,1,0:T(8,128)(2,1)S(1)}, u32[]{:S(2)}) copy-start(s16[4,128,256]{2,1,0:T(8,128)(2,1)S(1)} %collective-permute-done.20.refs_2_) | copy-start | bytes 786436
  248.6 11.5 %collective-permute-start.21 = (s16[4,128,256]{2,1,0:T(8,128)(2,1)S(1)}, s16[4,128,256]{2,1,0:T(8,128)(2,1)S(1)}, u32[]{:S(2)}, u32[]{:S(2)}) collective-permute-start(s16[4,128,256]{2,1,0:T(8,128)(2,1)S(1)} %copy-done.32), channel_id=1, source_target_pairs={{0,16},{1,17},{2,18},{3,19},{4,20},{5,21},{6,22},{7,23},{8,24},{9,... | collective-permute-start | bytes 786440 | tf_op jit(solution)/shard_map/ppermute | solution.py:44
  260.0 0.7 copy-start.14
  260.0 0.9 copy-start.5
  260.1 1.0 copy-start.6
  271.5 11.0 %copy-start.31 = (s16[3,128,512]{2,1,0:T(8,128)(2,1)S(1)}, s16[3,128,512]{2,1,0:T(8,128)(2,1)}, u32[]{:S(2)}) copy-start(s16[3,128,512]{2,1,0:T(8,128)(2,1)} %get-tuple-element.73) | copy-start | bytes 1179652
  271.5 17.2 %copy-start.30 = (s16[3,128,512]{2,1,0:T(8,128)(2,1)S(1)}, s16[3,128,512]{2,1,0:T(8,128)(2,1)}, u32[]{:S(2)}) copy-start(s16[3,128,512]{2,1,0:T(8,128)(2,1)} %get-tuple-element.74) | copy-start | bytes 1179652
  271.5 17.2 %copy-start = (s32[4]{0:T(128)S(1)}, s32[4]{0:T(128)}, u32[]{:S(2)}) copy-start(s32[4]{0:T(128)} %broadcast.48.refs_2_.which_ref) | copy-start | bytes 52
  271.5 28.2 %collective-permute-start.28 = (s16[3,128,512]{2,1,0:T(8,128)(2,1)}, s16[3,128,512]{2,1,0:T(8,128)(2,1)S(1)}, u32[]{:S(2)}, u32[]{:S(2)}) collective-permute-start(s16[3,128,512]{2,1,0:T(8,128)(2,1)} %get-tuple-element.72), channel_id=1, source_target_pairs={{0,64},{1,65},{2,66},{3,67},{4,68},{5,69},{6,70},{7,71},{8,72},{9,... | collective-permute-start | bytes 1179656 | tf_op jit(solution)/shard_map/ppermute | solution.py:44
  274.5 0.8 copy-start.7
  274.5 1.0 copy-start.8
  279.7 10.9 %collective-permute-start.13 = (s16[4,128,256]{2,1,0:T(8,128)(2,1)}, s16[4,128,256]{2,1,0:T(8,128)(2,1)S(1)}, u32[]{:S(2)}, u32[]{:S(2)}) collective-permute-start(s16[4,128,256]{2,1,0:T(8,128)(2,1)} %get-tuple-element.49), channel_id=1, source_target_pairs={{0,48},{1,49},{2,50},{3,51},{4,52},{5,53},{6,54},{7,55},{8,56},{9,... | collective-permute-start | bytes 786440 | tf_op jit(solution)/shard_map/ppermute | solution.py:44
  282.0 8.6 %collective-permute-start.14 = (s16[4,128,256]{2,1,0:T(8,128)(2,1)}, s16[4,128,256]{2,1,0:T(8,128)(2,1)S(1)}, u32[]{:S(2)}, u32[]{:S(2)}) collective-permute-start(s16[4,128,256]{2,1,0:T(8,128)(2,1)} %get-tuple-element.50), channel_id=1, source_target_pairs={{0,16},{1,17},{2,18},{3,19},{4,20},{5,21},{6,22},{7,23},{8,24},{9,... | collective-permute-start | bytes 786440 | tf_op jit(solution)/shard_map/ppermute | solution.py:44
  282.4 21.4 %collective-permute-start.29 = (s16[3,128,512]{2,1,0:T(8,128)(2,1)S(1)}, s16[3,128,512]{2,1,0:T(8,128)(2,1)S(1)}, u32[]{:S(2)}, u32[]{:S(2)}) collective-permute-start(s16[3,128,512]{2,1,0:T(8,128)(2,1)S(1)} %copy-done.31), channel_id=1, source_target_pairs={{0,8},{1,9},{2,10},{3,11},{4,12},{5,13},{6,14},{7,15},{8,0},{9,1},... | collective-permute-start | bytes 1179656 | tf_op jit(solution)/shard_map/ppermute | solution.py:44
  288.7 15.1 %collective-permute-start.30 = (s16[3,128,512]{2,1,0:T(8,128)(2,1)S(1)}, s16[3,128,512]{2,1,0:T(8,128)(2,1)S(1)}, u32[]{:S(2)}, u32[]{:S(2)}) collective-permute-start(s16[3,128,512]{2,1,0:T(8,128)(2,1)S(1)} %copy-done.30), channel_id=1, source_target_pairs={{0,72},{1,73},{2,74},{3,75},{4,76},{5,77},{6,78},{7,79},{8,64},{9,... | collective-permute-start | bytes 1179656 | tf_op jit(solution)/shard_map/ppermute | solution.py:44
  290.6 0.7 copy-start.15
  290.6 0.8 copy-start.16
  295.8 14.9 %collective-permute-start.15 = (s16[1,128,512]{2,1,0:T(8,128)(2,1)}, s16[1,128,512]{2,1,0:T(8,128)(2,1)S(1)}, u32[]{:S(2)}, u32[]{:S(2)}) collective-permute-start(s16[1,128,512]{2,1,0:T(8,128)(2,1)} %get-tuple-element.52), channel_id=1, source_target_pairs={{0,64},{1,65},{2,66},{3,67},{4,68},{5,69},{6,70},{7,71},{8,72},{9,... | collective-permute-start | bytes 393224 | tf_op jit(solution)/shard_map/ppermute | solution.py:44
  298.7 12.0 %collective-permute-start.16 = (s16[1,128,512]{2,1,0:T(8,128)(2,1)}, s16[1,128,512]{2,1,0:T(8,128)(2,1)S(1)}, u32[]{:S(2)}, u32[]{:S(2)}) collective-permute-start(s16[1,128,512]{2,1,0:T(8,128)(2,1)} %get-tuple-element.53), channel_id=1, source_target_pairs={{0,8},{1,9},{2,10},{3,11},{4,12},{5,13},{6,14},{7,15},{8,0},{9,1},... | collective-permute-start | bytes 393224 | tf_op jit(solution)/shard_map/ppermute | solution.py:44
  299.7 4.1 %copy-start.10 = (s16[3,128,512]{2,1,0:T(8,128)(2,1)}, s16[3,128,512]{2,1,0:T(8,128)(2,1)S(1)}, u32[]{:S(2)}) copy-start(s16[3,128,512]{2,1,0:T(8,128)(2,1)S(1)} %collective-permute-done.28.y_ref) | copy-start | bytes 1179652
  299.7 10.9 %collective-permute-start.17 = (s16[1,128,512]{2,1,0:T(8,128)(2,1)}, s16[1,128,512]{2,1,0:T(8,128)(2,1)S(1)}, u32[]{:S(2)}, u32[]{:S(2)}) collective-permute-start(s16[1,128,512]{2,1,0:T(8,128)(2,1)} %get-tuple-element.54), channel_id=1, source_target_pairs={{0,72},{1,73},{2,74},{3,75},{4,76},{5,77},{6,78},{7,79},{8,64},{9,... | collective-permute-start | bytes 393224 | tf_op jit(solution)/shard_map/ppermute | solution.py:44
  303.8 0.8 copy-start.11
  303.8 0.9 copy-start.12
  310.6 0.7 copy-start.17
  310.6 0.7 copy-start.18
  310.7 0.7 copy-start.19

commit v2 on v0

v2 whole, which is shorter than its diff:
```python
import jax
import jax.numpy as jnp
import numpy as np
from jax import lax
from jax.experimental import pallas as pl
from jax.experimental.pallas import tpu as pltpu
from jax.sharding import PartitionSpec as P

GENES = 8192
CELLS = 18432
AXES = ("cells", "grow", "gcol")
SIZES = (2, 4, 2, 4, 2)
ROWS = 1152
TILES = ROWS // 128
SPAN = 1024
HALF = 512
QUARTER = 256

ALPHA = 2.0**17 / 9.0e6
BETA = 32700.0 / float(np.log1p(2.0**17))
VMEM = 48 * 1024 * 1024


def moves(target):
    pairs = []
    for i, at in enumerate(np.ndindex(*SIZES)):
        to = tuple(v % s for v, s in zip(target(*at), SIZES))
        pairs.append((i, int(np.ravel_multi_index(to, SIZES))))
    return pairs


TO_CORE = moves(lambda h, z, c, x, b: (h, z, 1 - c, x, b))
TO_YLO = moves(lambda h, z, c, x, b: (h, z, c, x, 1 - b))
TO_YHI = moves(lambda h, z, c, x, b: (1 - h, z, c, x, b))
TO_YHI_CORE = moves(lambda h, z, c, x, b: (1 - h, z, 1 - c, x, b))
TO_X = [moves(lambda h, z, c, x, b, d=d: (h, z, c, x + d, b)) for d in (1, 2, 3)]
FIRST = (1, 3)
TO_Z_FIRST = moves(lambda h, z, c, x, b: (h, z ^ FIRST[c], c, x, b))
TO_Z_SECOND = moves(lambda h, z, c, x, b: (h, z ^ FIRST[1 - c], c, x, b))
TO_SAME = moves(lambda h, z, c, x, b: (h, z, c, x - 1 + 2 * c, b))
TO_CROSS = moves(lambda h, z, c, x, b: (h, z, 1 - c, x + 1 - 2 * c, b))

CORE, AWAY, KEEP, SEND, PLACE = 0, 1, 2, 4, 6


def table():
    rows = []
    for h, z, c, x, b in np.ndindex(*SIZES):
        row = [c, b ^ h]
        row += [(z ^ d) * QUARTER for d in (0, FIRST[1 - c], FIRST[c], 2)]
        for core in (c, 1 - c):
            near = (x + 1 - 2 * core) % 4
            chunks = ((x, core), (near, core), (near, 1 - core), (x ^ 2, core))
            row += [half * 16 + a for a, half in chunks]
        rows.append(row + [0] * 2)
    return np.array(rows, np.int32)


def send(value, pairs):
    return lax.ppermute(value, AXES, pairs)


def encode(total):
    size = jnp.log(1.0 + ALPHA * jnp.abs(total)) * BETA + 0.5
    code = size.astype(jnp.int32)
    return jnp.where(total < 0, -code, code).astype(jnp.int16)


def decode(code):
    code = code.astype(jnp.int32).astype(jnp.float32)
    size = (jnp.exp(jnp.abs(code) * (1.0 / BETA)) - 1.0) * (1.0 / ALPHA)
    return jnp.where(code < 0, -size, size)


def params(**_):
    return dict(
        compiler_params=pltpu.CompilerParams(vmem_limit_bytes=VMEM),
        cost_estimate=pl.CostEstimate(flops=30_000_000_000, bytes_accessed=1_000_000, transcendentals=0),
    )


def of(shape, dtype):
    return jax.ShapeDtypeStruct(shape, dtype)


STEPS = 3
PART = ROWS // STEPS
PART_TILES = PART // 128


def sums(counts, mean, scale):
    def body(counts_ref, mean_ref, scale_ref, out_ref):
        i = pl.program_id(0)

        @pl.when(i == 0)
        def _():
            inverse = 1.0 / scale_ref[...]
            out_ref[TILES : TILES + 8, :] = inverse
            out_ref[TILES + 8 : TILES + 16, :] = mean_ref[...] * inverse

        total = None
        for j in range(8):
            value = counts_ref[pl.ds(j, PART, stride=8), :]
            total = value if total is None else total + value
        total = total.astype(jnp.float32)
        for k in range(PART_TILES):
            across = jnp.sum(total[k * 128 : (k + 1) * 128, :].T, axis=0, keepdims=True)
            out_ref[pl.ds(i * PART_TILES + k, 1), :] = across

    whole = pl.BlockSpec((8, 128), lambda i: (0, 0))
    return pl.pallas_call(
        body,
        out_shape=of((TILES + 16, 128), jnp.float32),
        grid=(STEPS,),
        in_specs=[pl.BlockSpec((PART * 8, 128), lambda i: (i, 0)), whole, whole],
        out_specs=pl.BlockSpec((TILES + 16, 128), lambda i: (0, 0)),
        **params(byte=5 << 20),
    )(counts, mean, scale)


def narrow(counts, after):
    def body(counts_ref, after_ref, out_ref):
        for j in range(8):
            out_ref[:, j * 128 : (j + 1) * 128] = counts_ref[pl.ds(j, PART, stride=8), :].astype(jnp.int16)

    return pl.pallas_call(
        body,
        out_shape=of((ROWS, SPAN), jnp.int16),
        grid=(STEPS,),
        in_specs=[pl.BlockSpec((PART * 8, 128), lambda i: (i, 0)), pl.BlockSpec(memory_space=pl.ANY)],
        out_specs=pl.BlockSpec((PART, SPAN), lambda i: (i, 0)),
        **params(byte=8 << 20),
    )(counts, after)


def join(part, part_y, after):
    def body(part_ref, y_ref, after_ref, out_ref):
        out_ref[0:TILES, :] = part_ref[0:TILES, :] + y_ref[0:TILES, :]
        out_ref[TILES:, :] = part_ref[TILES:, :]

    small = pl.BlockSpec(memory_space=pltpu.VMEM)
    return pl.pallas_call(
        body,
        out_shape=of(part.shape, part.dtype),
        in_specs=[small, small, pl.BlockSpec(memory_space=pl.ANY)],
        out_specs=small,
        **params(),
    )(part, part_y, after)


def halves(where, block, after):
    def body(where_ref, first_in, other_in, after_ref, first_ref, other_ref):
        first_ref[...] = first_in[...]
        other_ref[...] = other_in[...]

    half = pl.BlockSpec((PART, HALF), lambda i, w: (i, 0))
    return pl.pallas_call(
        body,
        out_shape=(of((ROWS, HALF), block.dtype),) * 2,
        grid_spec=pltpu.PrefetchScalarGridSpec(
            num_scalar_prefetch=1,
            grid=(STEPS,),
            in_specs=[
                pl.BlockSpec((PART, HALF), lambda i, w: (i, w[CORE])),
                pl.BlockSpec((PART, HALF), lambda i, w: (i, 1 - w[CORE])),
                pl.BlockSpec(memory_space=pl.ANY),
            ],
            out_specs=[half, half],
        ),
        **params(byte=5 << 20),
    )(where, block, block, after)


def factors(total_refs, i):
    tiles = []
    for k in range(PART_TILES):
        row = sum(ref[pl.ds(i * PART_TILES + k, 1), :] for ref in total_refs)
        tiles.append(jnp.broadcast_to(GENES / row, (128, 128)).T)
    return jnp.concatenate(tiles, axis=0)


def standardized(count, factor, inverse, shift):
    value = count.astype(jnp.int32).astype(jnp.float32)
    return (jnp.log(1.0 + value * factor) * inverse - shift).astype(jnp.bfloat16)


SMALL = (TILES + 16, 128)


def standardize(where, counts, totals, gene, after, split):
    n = len(totals)

    def body(where_ref, counts_ref, *refs):
        gene_ref, after_ref, out_ref = refs[n : n + 3]
        half = pl.program_id(1)
        factor = factors(refs[:n], pl.program_id(0))

        def run(*out_refs):
            for j in range(4):
                lanes = slice(j * 128, (j + 1) * 128)
                at = TILES + half * 4 + j
                inverse, shift = gene_ref[pl.ds(at, 1), :], gene_ref[pl.ds(at + 8, 1), :]
                value = standardized(counts_ref[:, lanes], factor, inverse, shift)
                for ref in out_refs:
                    ref[:, lanes] = value

        if split:
            first_ref, other_ref = refs[n + 3 :]

            @pl.when(half == where_ref[CORE])
            def _():
                run(out_ref, first_ref)

            @pl.when(half != where_ref[CORE])
            def _():
                run(out_ref, other_ref)

        else:
            run(out_ref)

    small = pl.BlockSpec(SMALL, lambda i, h, w: (0, 0))
    rows = pl.BlockSpec((TILES, 128), lambda i, h, w: (0, 0))
    block = pl.BlockSpec((PART, HALF), lambda i, h, w: (i, h))
    half = pl.BlockSpec((PART, HALF), lambda i, h, w: (i, 0))
    whole = of((ROWS, SPAN), jnp.bfloat16)
    halved = (of((ROWS, HALF), jnp.bfloat16),) * 2
    return pl.pallas_call(
        body,
        out_shape=(whole, *halved) if split else whole,
        grid_spec=pltpu.PrefetchScalarGridSpec(
            num_scalar_prefetch=1,
            grid=(STEPS, 2),
            in_specs=[block] + [rows] * n + [small] + [pl.BlockSpec(memory_space=pl.ANY)],
            out_specs=[block, half, half] if split else block,
        ),
        **params(byte=7 << 20),
    )(where, counts, *totals, gene, after)


def standardize_near(where, mine, sibling, total, total_sibling, right, left):
    def body(where_ref, mine_ref, sibling_ref, t_ref, ts_ref, right_ref, left_ref, out_ref):
        i = pl.program_id(0)
        core = where_ref[CORE]

        def run(count_ref, total_ref, gene_ref):
            factor = factors([total_ref], i % STEPS)
            for j in range(4):
                lanes = slice(j * 128, (j + 1) * 128)
                at = TILES + core * 4 + j
                inverse, shift = gene_ref[pl.ds(at, 1), :], gene_ref[pl.ds(at + 8, 1), :]
                out_ref[:, lanes] = standardized(count_ref[:, lanes], factor, inverse, shift)

        for part, count_ref, total_ref in ((0, mine_ref, t_ref), (1, sibling_ref, ts_ref)):
            for side, gene_ref in ((0, right_ref), (1, left_ref)):

                @pl.when((i // STEPS == part) & (core == side))
                def _():
                    run(count_ref, total_ref, gene_ref)

    small = pl.BlockSpec(SMALL, lambda i, w: (0, 0))
    rows = pl.BlockSpec((TILES, 128), lambda i, w: (0, 0))
    return pl.pallas_call(
        body,
        out_shape=of((2 * ROWS, HALF), jnp.bfloat16),
        grid_spec=pltpu.PrefetchScalarGridSpec(
            num_scalar_prefetch=1,
            grid=(2 * STEPS,),
            in_specs=[
                pl.BlockSpec((PART, HALF), lambda i, w: (jnp.minimum(i, STEPS - 1), 0)),
                pl.BlockSpec((PART, HALF), lambda i, w: (jnp.maximum(i - STEPS, 0), 0)),
                rows,
                rows,
                small,
                small,
            ],
            out_specs=pl.BlockSpec((PART, HALF), lambda i, w: (i, 0)),
        ),
        **params(byte=5 << 20),
    )(where, mine, sibling, total, total_sibling, right, left)


def products(where, rows, cols, after):
    n_rows, n_cols = len(rows), len(cols)
    units = max(n_rows, n_cols)
    flat = [a for block in rows + cols for a in block]

    def body(where_ref, *refs):
        sources = refs[: len(flat)]
        go_ref, stay_ref, rows_v, cols_v, *product, sems = refs[len(flat) + 1 :]
        step = pl.program_id(0)
        core = where_ref[CORE]

        def copies(unit):
            which = []
            k = 0
            for b, block in enumerate(rows + cols):
                place, u = (rows_v, b) if b < n_rows else (cols_v, b - n_rows)
                for part in range(len(block)):
                    if u == unit:
                        source = sources[k]
                        size = source.shape[0]
                        if b >= n_rows and source.shape[1] == SPAN:
                            source = source.at[:, pl.ds(pl.multiple_of(core * HALF, HALF), HALF)]
                        target = place.at[u, pl.ds(part * size, size)]
                        which.append(pltpu.make_async_copy(source, target, sems.at[k]))
                    k += 1
            return which

        @pl.when(step == 0)
        def _():
            for unit in range(units):
                for c in copies(unit):
                    c.start()

        for unit in range(units):

            @pl.when(step == unit)
            def _():
                for c in copies(unit):
                    c.wait()

        r = step if n_rows > 1 else 0
        q = step if n_cols > 1 else 0
        for tile in range(2):
            lanes = slice(tile * 256, tile * 256 + 256)
            product[tile][...] = lax.dot_general(
                rows_v[r], cols_v[q, :, lanes], (((0,), (0,)), ((), ())), preferred_element_type=jnp.float32
            )
            for k in range(2):
                at = pl.multiple_of(where_ref[KEEP + k], QUARTER)
                stay_ref[0, k, :, lanes] = product[tile][pl.ds(at, QUARTER), :]
                at = pl.multiple_of(where_ref[SEND + k], QUARTER)
                go_ref[0, k, :, lanes] = encode(product[tile][pl.ds(at, QUARTER), :])

    out = pl.BlockSpec((1, 2, QUARTER, HALF), lambda i, w: (i, 0, 0, 0))
    return pl.pallas_call(
        body,
        out_shape=(of((units, 2, QUARTER, HALF), jnp.int16), of((units, 2, QUARTER, HALF), jnp.float32)),
        grid_spec=pltpu.PrefetchScalarGridSpec(
            num_scalar_prefetch=1,
            grid=(units,),
            in_specs=[pl.BlockSpec(memory_space=pltpu.HBM)] * len(flat) + [pl.BlockSpec(memory_space=pl.ANY)],
            out_specs=[out, out],
            scratch_shapes=[
                pltpu.VMEM((n_rows, 2 * ROWS, SPAN), jnp.bfloat16),
                pltpu.VMEM((n_cols, 2 * ROWS, HALF), jnp.bfloat16),
                pltpu.VMEM((SPAN, 256), jnp.float32),
                pltpu.VMEM((SPAN, 256), jnp.float32),
                pltpu.SemaphoreType.DMA((len(flat),)),
            ],
        ),
        **params(flops=2 * units * SPAN * HALF * 2 * ROWS, byte=6 * units << 20),
    )(where, *flat, after)


def second(stay, got):
    units = stay.shape[0]

    def body(stay_ref, got_ref, go_ref, out_ref):
        out_ref[0] = stay_ref[0, 0] + decode(got_ref[0, 0])
        go_ref[0] = encode(stay_ref[0, 1] + decode(got_ref[0, 1]))

    four = pl.BlockSpec((1, 2, QUARTER, HALF), lambda i: (i, 0, 0, 0))
    three = pl.BlockSpec((1, QUARTER, HALF), lambda i: (i, 0, 0))
    return pl.pallas_call(
        body,
        grid=(units,),
        out_shape=(of((units, QUARTER, HALF), jnp.int16), of((units, QUARTER, HALF), jnp.float32)),
        in_specs=[four, four],
        out_specs=[three, three],
        **params(byte=5 << 20),
    )(stay, got)


def summed_z(where, chunks, own, other):
    parts = own + other

    def body(where_ref, *refs):
        keep, to_c, to_y, to_yc, total = refs[2 * len(parts) :]
        i = pl.program_id(0)
        for p, (_, _, which) in enumerate(parts):
            held = [k for k in range(chunks) if which[k] is not None]
            side = 0 if p < len(own) else 1

            @pl.when((i >= held[0]) & (i <= held[-1]))
            def _():
                total[side] = refs[2 * p][0] + decode(refs[2 * p + 1][0])

        near, far = where_ref[AWAY], 1 - where_ref[AWAY]
        mine = pl.ds(pl.multiple_of(where_ref[CORE] * 128, 128), 128)
        others = pl.ds(pl.multiple_of((1 - where_ref[CORE]) * 128, 128), 128)
        keep[0] = total[near, mine, :]
        to_c[0] = encode(total[near, others, :])
        to_y[0] = encode(total[far, mine, :])
        to_yc[0] = encode(total[far, others, :])

    def at(which):
        held = [(k, u) for k, u in enumerate(which) if u is not None]
        first, base = held[0]
        return lambda i, w: (jnp.clip(i - first, 0, len(held) - 1) + base, 0, 0)

    in_specs, operands = [], []
    for stay, got, which in parts:
        in_specs += [pl.BlockSpec((1, QUARTER, HALF), at(which))] * 2
        operands += [stay, got]
    return pl.pallas_call(
        body,
        out_shape=(of((chunks, 128, HALF), jnp.float32),) + (of((chunks, 128, HALF), jnp.int16),) * 3,
        grid_spec=pltpu.PrefetchScalarGridSpec(
            num_scalar_prefetch=1,
            grid=(chunks,),
            in_specs=in_specs,
            out_specs=[pl.BlockSpec((1, 128, HALF), lambda i, w: (i, 0, 0))] * 4,
            scratch_shapes=[pltpu.VMEM((2, QUARTER, HALF), jnp.float32)],
        ),
        **params(byte=chunks * (2 << 20)),
    )(where, *operands)


def finish(where, keep, got_c, got_y, got_yc, chunk, out=None):
    n = keep.shape[0]

    def body(where_ref, keep_ref, c_ref, y_ref, yc_ref, *rest):
        out_ref = rest[-1]
        i = pl.program_id(0)
        if out is not None:

            @pl.when(i == 0)
            def _():
                out_ref[...] = rest[0][...]

        mine = (keep_ref[0] + decode(y_ref[0])) * (1.0 / CELLS)
        others = (decode(c_ref[0]) + decode(yc_ref[0])) * (1.0 / CELLS)
        for place, value in ((PLACE, mine), (PLACE + 4, others)):
            base = where_ref[place + chunk + i]
            for q in range(4):
                out_ref[pl.ds(base + 4 * q, 128, stride=32), :] = value[:, q * 128 : (q + 1) * 128]

    block = pl.BlockSpec((1, 128, HALF), lambda i, w: (i, 0, 0))
    whole = pl.BlockSpec((4096, 128), lambda i, w: (0, 0))
    in_specs, operands, alias = [block] * 4, [keep, got_c, got_y, got_yc], {}
    if out is not None:
        in_specs.append(whole)
        operands.append(out)
        alias = {5: 0}
    return pl.pallas_call(
        body,
        out_shape=of((4096, 128), jnp.float32),
        grid_spec=pltpu.PrefetchScalarGridSpec(
            num_scalar_prefetch=1, grid=(n,), in_specs=in_specs, out_specs=whole
        ),
        input_output_aliases=alias,
        **params(byte=4 << 20),
    )(where, *operands)


def exchange_z(go, stay):
    go, stay = second(stay, send(go, TO_Z_FIRST))
    return stay, send(go, TO_Z_SECOND)


def per_device(counts, gene_mean, gene_scale):
    device = (lax.axis_index("cells") * 4 + lax.axis_index("grow")) * 2 + lax.axis_index("gcol")
    where = lax.dynamic_slice(jnp.asarray(table()), (device, 0), (1, 16)).reshape(16)
    counts = counts.reshape(ROWS * 8, 128)

    part = sums(counts, gene_mean.reshape(8, 128), gene_scale.reshape(8, 128))
    part_y = send(part, TO_YLO)
    whole = narrow(counts, part)
    y_counts = send(whole, TO_YLO)
    pair = join(part, part_y, whole)
    left, opposite, right = [send(pair, to) for to in TO_X]
    first, other = halves(where, whole, pair)
    n0 = send(first, TO_SAME), send(other, TO_CROSS)
    total = pair[:TILES] + left[:TILES] + opposite[:TILES] + right[:TILES]
    total_sibling = send(total, TO_CORE)

    own, first, other = standardize(where, whole, [total], part, total, True)
    own = own, send(own, TO_CORE)
    n1 = send(other, TO_SAME), send(first, TO_CROSS)
    n0 = (standardize_near(where, *n0, total, total_sibling, right, left),)
    x2 = (send(n0[0], TO_SAME),)

    go, stay = products(where, [own], [own, n0], total)
    round_1 = exchange_z(go, stay)
    go, stay = products(where, [own], [n1], go)
    round_2 = exchange_z(go, stay)
    y = standardize(where, y_counts, [total], part_y, go, False)
    y = y, send(y, TO_CORE)
    go, stay = products(where, [y], [own, n0, n1], go)
    round_3 = exchange_z(go, stay)
    go, stay = products(where, [own, y], [x2], go)
    round_4 = exchange_z(go, stay)

    keep, to_c, to_y, to_yc = summed_z(
        where,
        3,
        [(*round_1, [0, 1, None]), (*round_2, [None, None, 0])],
        [(*round_3, [0, 1, 2])],
    )
    out = finish(where, keep, send(to_c, TO_CORE), send(to_y, TO_YHI), send(to_yc, TO_YHI_CORE), 0)
    keep, to_c, to_y, to_yc = summed_z(where, 1, [(*round_4, [0])], [(*round_4, [1])])
    out = finish(where, keep, send(to_c, TO_CORE), send(to_y, TO_YHI), send(to_yc, TO_YHI_CORE), 3, out)
    return out.reshape(128, 8, 4, 128).transpose(0, 2, 1, 3).reshape(1, 128, 1, 4, SPAN)


def solution(mesh):
    placed = (P("cells", "grow", "gcol", None), P("grow", "gcol", None), P("grow", "gcol", None))
    return jax.shard_map(
        per_device,
        mesh=mesh,
        in_specs=placed,
        out_specs=P("grow", "cells", "gcol", None, None),
        check_vma=False,
    )
```

time: 497 us -> 194 us (0.39)
  waiting for transfers between devices: 403 us -> 59.9 us
  Pallas kernels: 0 us -> 85.1 us
  starting transfers between devices: 0.08 us -> 42.9 us
  matrix products: 29 us -> 0 us
  blocking collectives: 17.1 us -> 0 us
  local copies, waits for them, and re-layouts: 21.8 us -> 5.56 us
  between operations: 13.1 us -> 0.23 us
  other arithmetic: 10.4 us -> 0.01 us
    reduce_scatter x1 -> x0, waiting for transfers between devices: 246 us -> none  [per_device(): lax.psum_scatter(lax.dot_general(row_flat, col_flat, (((0,), (0,)), ((),...]
    all_gather x2 -> x0, waiting for transfers between devices: 156 us -> none  [the longest x1 87.9 us: per_device(): lax.all_gather(standard.reshape(cell_rows, 1, width), 'grow', axis=1, til...]
    pallas_call x0 -> x19, Pallas kernels: none -> 85.1 us  [the longest x4 40.3 us: products(): pl.pallas_call(body, out_shape=(of((units, 2, QUARTER, HALF), jnp.int16),...]
    ppermute x0 -> x27, waiting for transfers between devices: none -> 59.9 us  [send(): return lax.ppermute(value, AXES, pairs)]
    ppermute x0 -> x27, starting transfers between devices: none -> 42.9 us  [send(): return lax.ppermute(value, AXES, pairs)]
    dot_general x1 -> x0, matrix products: 29 us -> none  [per_device(): lax.dot_general(row_flat, col_flat, (((0,), (0,)), ((), ())), preferred_e...]
    all_gather x2 -> x0, local copies, waits for them, and re-layouts: 19.4 us -> none  [the longest x1 12.6 us: per_device(): lax.all_gather(standard.reshape(cell_rows, 1, width), 'grow', axis=1, til...]
    psum x1 -> x0, blocking collectives: 17.1 us -> none  [per_device(): totals = lax.psum(partial_totals, ('grow', 'gcol'))]
  transfers between devices with their start and end apart: 3 -> 27, of which waited for: 3 -> 11; matrix products, arithmetic and copies ran while one was open for 1% -> 0% of each run, Pallas kernels for 0% -> 41%
where the time goes in v2:
time: 194 us
  Pallas kernels  85.1 us (44%)
  waiting for transfers between devices  59.9 us (31%)
  starting transfers between devices  42.9 us (22%)
  local copies, waits for them, and re-layouts  5.56 us (3%)
    ppermute x27, waiting for transfers between devices, send(): return lax.ppermute(value, AXES, pairs)  59.9 us
    ppermute x27, starting transfers between devices, send(): return lax.ppermute(value, AXES, pairs)  42.9 us
    pallas_call x4, Pallas kernels, products(): pl.pallas_call(body, out_shape=(of((units, 2, QUARTER, HALF), jnp.int16),...  40.3 us
    pallas_call x2, Pallas kernels, standardize(): pl.pallas_call(body, out_shape=(whole, *halved) if split else whole, grid...  10.2 us
    pallas_call x2, Pallas kernels, finish(): pl.pallas_call(body, out_shape=of((4096, 128), jnp.float32), grid_spec=pl...  8.16 us
    pallas_call x4, Pallas kernels, second(): pl.pallas_call(body, grid=(units,), out_shape=(of((units, QUARTER, HALF),...  7.44 us
    pallas_call x2, Pallas kernels, summed_z(): pl.pallas_call(body, out_shape=(of((chunks, 128, HALF), jnp.float32),) +...  6.01 us
    pallas_call x1, Pallas kernels, narrow(): pl.pallas_call(body, out_shape=of((ROWS, SPAN), jnp.int16), grid=(STEPS,)...  5.05 us
  transfers between devices with their start and end apart: 27, of which 11 were waited for; matrix products, arithmetic and copies ran while one was open for 0% of the time, Pallas kernels for 41%

profile of v2, /device:TPU:1, one launch (start us, length us, event | category | flops | bytes accessed | tf_op | source)
XLA Modules:
  0.0 193.7 jit_solution(9780929394128909081)
XLA Ops:
  0.0 2.3 %copy-done = s32[1152,1,1,1024]{3,2,1,0:T(1,128)S(1)} copy-done((s32[1152,1,1,1024]{3,2,1,0:T(1,128)S(1)}, s32[1152,1,1,1024]{3,2,1,0:T(1,128)}, u32[]{:S(2)}) %copy-start) | copy-done | bytes 4718616
  2.3 0.7 copy-done.5
  3.0 0.7 copy-done.6
  3.7 0.9 shard_map.46.after_ref.part_ref.refs_1_
  4.6 2.2 %collective-permute-start = (f32[25,128]{1,0:T(8,128)S(1)}, f32[25,128]{1,0:T(8,128)S(1)}, u32[]{:S(2)}, u32[]{:S(2)}) collective-permute-start(f32[25,128]{1,0:T(8,128)S(1)} %shard_map.46.after_ref.part_ref.refs_1_), channel_id=1, source_target_pairs={{0,1},{1,0},{2,3},{3,2},{4,5},{5,4},{6,7},{7,6},{8,9},{9,8},{10,11... | collective-permute-start | bytes 38408 | tf_op jit(solution)/shard_map/ppermute | solution.py:60
  6.8 5.1 %shard_map.47.after_ref.counts_ref.first_in.other_in = s16[1152,1024]{1,0:T(8,128)(2,1)} custom-call(s32[9216,128]{1,0:T(8,128)} %bitcast.10, f32[25,128]{1,0:T(8,128)S(1)} %shard_map.46.after_ref.part_ref.refs_1_), custom_call_target="tpu_custom_call" | custom-call | flops 30000001024 | bytes 1000000 | tf_op jit(solution)/shard_map/pallas_call | solution.py:126
  11.8 0.0 collective-permute-start.5
  11.9 0.7 dynamic-slice_bitcast_fusion.where_ref
  12.6 0.6 copy-done.3
  13.2 2.6 %collective-permute-start.3 = (f32[25,128]{1,0:T(8,128)S(1)}, f32[25,128]{1,0:T(8,128)S(1)}, u32[]{:S(2)}, u32[]{:S(2)}) collective-permute-start(f32[25,128]{1,0:T(8,128)S(1)} %shard_map.48.after_ref), channel_id=1, source_target_pairs={{0,6},{1,7},{2,0},{3,1},{4,2},{5,3},{6,4},{7,5},{8,14},{9,15},{10,... | collective-permute-start | bytes 38408 | tf_op jit(solution)/shard_map/ppermute | solution.py:60
  15.8 0.5 collective-permute-start.2
  16.3 0.6 collective-permute-start.1
  16.9 3.0 %shard_map.50 = (s16[1152,512]{1,0:T(8,128)(2,1)S(1)}, s16[1152,512]{1,0:T(8,128)(2,1)S(1)}) custom-call(s32[16]{0:T(128)S(1)} %dynamic-slice_bitcast_fusion.where_ref, s16[1152,1024]{1,0:T(8,128)(2,1)} %shard_map.47.after_ref.counts_ref.first_in.other_in, s16[1152,1024]{1,0:T(8,128)(2,1)} %shard_map.47.after_ref.counts_ref.first_in.other_in, ...), custom_call_target="tpu_custom_call" | custom-call | flops 30000001024 | bytes 1000000 | tf_op jit(solution)/shard_map/pallas_call | solution.py:157
  19.9 1.6 collective-permute-start.8
  21.5 0.0 collective-permute-done.3.right_ref
  21.5 2.6 %collective-permute-start.9 = (s16[1152,512]{1,0:T(8,128)(2,1)S(1)}, s16[1152,512]{1,0:T(8,128)(2,1)S(1)}, u32[]{:S(2)}, u32[]{:S(2)}) collective-permute-start(s16[1152,512]{1,0:T(8,128)(2,1)S(1)} %get-tuple-element.38), channel_id=1, source_target_pairs={{0,10},{1,11},{2,12},{3,13},{4,14},{5,15},{6,8},{7,9},{8,6},{9,7},... | collective-permute-start | bytes 3538952 | tf_op jit(solution)/shard_map/ppermute | solution.py:60
  24.1 0.4 collective-permute-start.10
  24.5 5.3 %shard_map.49 = (bf16[1152,1024]{1,0:T(8,128)(2,1)S(1)}, bf16[1152,512]{1,0:T(8,128)(2,1)S(1)}, bf16[1152,512]{1,0:T(8,128)(2,1)S(1)}) custom-call(s32[16]{0:T(128)S(1)} %dynamic-slice_bitcast_fusion.where_ref, s16[1152,1024]{1,0:T(8,128)(2,1)} %shard_map.47.after_ref.counts_ref.first_in.other_in, f32[9,128]{1,0:T(8,128)S(1)} %slice_add_fusion.refs_0_.refs_2_.t_ref.refs_5_, ...), custom_call_target="tpu_custom_call" | custom-call | flops 30000001024 | bytes 1000000 | tf_op jit(solution)/shard_map/pallas_call | solution.py:227
  29.8 1.4 collective-permute-start.6
  31.2 0.7 collective-permute-start.7
  31.9 14.8 %collective-permute-done.8.mine_ref = s16[1152,512]{1,0:T(8,128)(2,1)S(1)} collective-permute-done((s16[1152,512]{1,0:T(8,128)(2,1)S(1)}, s16[1152,512]{1,0:T(8,128)(2,1)S(1)}, u32[]{:S(2)}, u32[]{:S(2)}) %collective-permute-start.8) | collective-permute-done | bytes 1179680 | tf_op jit(solution)/shard_map/ppermute | solution.py:60
  46.7 4.0 %collective-permute-start.4 = (bf16[1152,1024]{1,0:T(8,128)(2,1)S(1)}, bf16[1152,1024]{1,0:T(8,128)(2,1)}, u32[]{:S(2)}, u32[]{:S(2)}) collective-permute-start(bf16[1152,1024]{1,0:T(8,128)(2,1)S(1)} %get-tuple-element.34.refs_0_.refs_2_), channel_id=1, source_target_pairs={{0,8},{1,9},{2,10},{3,11},{4,12},{5,13},{6,14},{7,15},{8,0},{9,1},... | collective-permute-start | bytes 7077896 | tf_op jit(solution)/shard_map/ppermute | solution.py:60
  50.7 0.4 collective-permute-done.9.sibling_ref
  51.0 4.1 %shard_map.51.refs_4_ = bf16[2304,512]{1,0:T(8,128)(2,1)} custom-call(s32[16]{0:T(128)S(1)} %dynamic-slice_bitcast_fusion.where_ref, s16[1152,512]{1,0:T(8,128)(2,1)S(1)} %collective-permute-done.8.mine_ref, s16[1152,512]{1,0:T(8,128)(2,1)S(1)} %collective-permute-done.9.sibling_ref, f32[9,128]{1,0:T(8,128)S(1)} %slice_add_fusion.refs_0_.refs_2_.t_ref.refs_5_, ...), custom_call_target="tpu_custom_call" | custom-call | flops 30000001024 | bytes 1000000 | tf_op jit(solution)/shard_map/pallas_call | solution.py:262
  55.2 1.7 collective-permute-start.12
  56.9 9.4 %shard_map.52 = (s16[2,2,256,512]{3,2,1,0:T(8,128)(2,1)S(1)}, f32[2,2,256,512]{3,2,1,0:T(8,128)S(1)}) custom-call(s32[16]{0:T(128)S(1)} %dynamic-slice_bitcast_fusion.where_ref, bf16[1152,1024]{1,0:T(8,128)(2,1)S(1)} %get-tuple-element.34.refs_0_.refs_2_, bf16[1152,1024]{1,0:T(8,128)(2,1)} %collective-permute-done.4.refs_1_.refs_3_, ...), custom_call_target="tpu_custom_call" | custom-call | flops 30000001024 | bytes 1000000 | tf_op jit(solution)/shard_map/pallas_call | solution.py:336
  66.3 0.0 copy-start.7
  66.3 4.0 %collective-permute-start.18 = (s16[2,2,256,512]{3,2,1,0:T(8,128)(2,1)S(1)}, s16[2,2,256,512]{3,2,1,0:T(8,128)(2,1)S(1)}, u32[]{:S(2)}, u32[]{:S(2)}) collective-permute-start(s16[2,2,256,512]{3,2,1,0:T(8,128)(2,1)S(1)} %get-tuple-element.39.refs_4_), channel_id=1, source_target_pairs={{0,16},{1,17},{2,18},{3,19},{4,20},{5,21},{6,22},{7,23},{8,56},{9,... | collective-permute-start | bytes 3145736 | tf_op jit(solution)/shard_map/ppermute | solution.py:60
  70.3 1.7 collective-permute-done.6.refs_2_.refs_5_
  72.0 4.3 %collective-permute-done.7.refs_3_.refs_6_ = bf16[1152,512]{1,0:T(8,128)(2,1)S(1)} collective-permute-done((bf16[1152,512]{1,0:T(8,128)(2,1)S(1)}, bf16[1152,512]{1,0:T(8,128)(2,1)S(1)}, u32[]{:S(2)}, u32[]{:S(2)}) %collective-permute-start.7) | collective-permute-done | bytes 1179680 | tf_op jit(solution)/shard_map/ppermute | solution.py:60
  76.3 6.3 %shard_map.53 = (s16[1,2,256,512]{3,2,1,0:T(8,128)(2,1)S(1)}, f32[1,2,256,512]{3,2,1,0:T(8,128)S(1)}) custom-call(s32[16]{0:T(128)S(1)} %dynamic-slice_bitcast_fusion.where_ref, bf16[1152,1024]{1,0:T(8,128)(2,1)} %copy-done.1, bf16[1152,1024]{1,0:T(8,128)(2,1)} %collective-permute-done.4.refs_1_.refs_3_, ...), custom_call_target="tpu_custom_call" | custom-call | flops 30000001024 | bytes 1000000 | tf_op jit(solution)/shard_map/pallas_call | solution.py:336
  82.6 3.8 %collective-permute-start.20 = (s16[1,2,256,512]{3,2,1,0:T(8,128)(2,1)S(1)}, s16[1,2,256,512]{3,2,1,0:T(8,128)(2,1)S(1)}, u32[]{:S(2)}, u32[]{:S(2)}) collective-permute-start(s16[1,2,256,512]{3,2,1,0:T(8,128)(2,1)S(1)} %get-tuple-element.40.refs_2_.refs_7_), channel_id=1, source_target_pairs={{0,16},{1,17},{2,18},{3,19},{4,20},{5,21},{6,22},{7,23},{8,56},{9,... | collective-permute-start | bytes 1572872 | tf_op jit(solution)/shard_map/ppermute | solution.py:60
  86.4 4.9 %shard_map.54.refs_0_.refs_2_ = bf16[1152,1024]{1,0:T(8,128)(2,1)S(1)} custom-call(s32[16]{0:T(128)S(1)} %dynamic-slice_bitcast_fusion.where_ref, s16[1152,1024]{1,0:T(8,128)(2,1)} %collective-permute-done.5.counts_ref, f32[9,128]{1,0:T(8,128)S(1)} %slice_add_fusion.refs_0_.refs_2_.t_ref.refs_5_, f32[25,128]{1,0:T(8,128)S(1)} %copy-done.4, ...), custom_call_target="tpu_custom_call" | custom-call | flops 30000001024 | bytes 1000000 | tf_op jit(solution)/shard_map/pallas_call | solution.py:227
  91.3 0.1 collective-permute-start.11
  91.4 1.6 collective-permute-done.20.got_ref
  93.0 1.1 shard_map.60
  94.2 0.5 copy-done.8
  94.7 1.3 shard_map.59
  96.0 1.0 collective-permute-start.19
  97.0 14.3 %shard_map.55 = (s16[3,2,256,512]{3,2,1,0:T(8,128)(2,1)S(1)}, f32[3,2,256,512]{3,2,1,0:T(8,128)}) custom-call(s32[16]{0:T(128)S(1)} %dynamic-slice_bitcast_fusion.where_ref, bf16[1152,1024]{1,0:T(8,128)(2,1)} %copy-done.2, bf16[1152,1024]{1,0:T(8,128)(2,1)} %collective-permute-done.11.refs_1_.refs_3_, bf16[1152,1024]{1,0:T(8,128)(2,1)} %copy-done.1, ...), custom_call_target="tpu_custom_call" | custom-call | flops 30000001024 | bytes 1000000 | tf_op jit(solution)/shard_map/pallas_call | solution.py:336
  111.3 3.0 %collective-permute-start.22 = (s16[3,2,256,512]{3,2,1,0:T(8,128)(2,1)S(1)}, s16[3,2,256,512]{3,2,1,0:T(8,128)(2,1)S(1)}, u32[]{:S(2)}, u32[]{:S(2)}) collective-permute-start(s16[3,2,256,512]{3,2,1,0:T(8,128)(2,1)S(1)} %get-tuple-element.41.refs_5_), channel_id=1, source_target_pairs={{0,16},{1,17},{2,18},{3,19},{4,20},{5,21},{6,22},{7,23},{8,56},{9,... | collective-permute-start | bytes 4718600 | tf_op jit(solution)/shard_map/ppermute | solution.py:60
  114.3 10.3 %shard_map.56 = (s16[2,2,256,512]{3,2,1,0:T(8,128)(2,1)S(1)}, f32[2,2,256,512]{3,2,1,0:T(8,128)S(1)}) custom-call(s32[16]{0:T(128)S(1)} %dynamic-slice_bitcast_fusion.where_ref, bf16[1152,1024]{1,0:T(8,128)(2,1)} %copy-done.1, bf16[1152,1024]{1,0:T(8,128)(2,1)} %collective-permute-done.4.refs_1_.refs_3_, bf16[1152,1024]{1,0:T(8,128)(2,1)} %copy-done.2, ...), custom_call_target="tpu_custom_call" | custom-call | flops 30000001024 | bytes 1000000 | tf_op jit(solution)/shard_map/pallas_call | solution.py:336
  124.6 0.1 collective-permute-start.13
  124.7 7.4 %collective-permute-done.22.got_ref = s16[3,2,256,512]{3,2,1,0:T(8,128)(2,1)S(1)} collective-permute-done((s16[3,2,256,512]{3,2,1,0:T(8,128)(2,1)S(1)}, s16[3,2,256,512]{3,2,1,0:T(8,128)(2,1)S(1)}, u32[]{:S(2)}, u32[]{:S(2)}) %collective-permute-start.22) | collective-permute-done | bytes 1572896 | tf_op jit(solution)/shard_map/ppermute | solution.py:60
  132.1 3.7 %shard_map.61 = (s16[3,256,512]{2,1,0:T(8,128)(2,1)S(1)}, f32[3,256,512]{2,1,0:T(8,128)S(1)}) custom-call(f32[3,2,256,512]{3,2,1,0:T(8,128)} %get-tuple-element.56.stay_ref, s16[3,2,256,512]{3,2,1,0:T(8,128)(2,1)S(1)} %collective-permute-done.22.got_ref), custom_call_target="tpu_custom_call" | custom-call | flops 30000001024 | bytes 1000000 | tf_op jit(solution)/shard_map/pallas_call | solution.py:365
  135.9 0.0 copy-start.9
  135.9 0.3 collective-permute-start.23
  136.2 7.2 %collective-permute-done.13.got_ref = s16[2,2,256,512]{3,2,1,0:T(8,128)(2,1)S(1)} collective-permute-done((s16[2,2,256,512]{3,2,1,0:T(8,128)(2,1)S(1)}, s16[2,2,256,512]{3,2,1,0:T(8,128)(2,1)S(1)}, u32[]{:S(2)}, u32[]{:S(2)}) %collective-permute-start.13) | collective-permute-done | bytes 1048608 | tf_op jit(solution)/shard_map/ppermute | solution.py:60
  143.3 1.3 shard_map.57
  144.6 1.3 collective-permute-start.14
  145.9 8.7 %collective-permute-done.23.refs_5_ = s16[3,256,512]{2,1,0:T(8,128)(2,1)S(1)} collective-permute-done((s16[3,256,512]{2,1,0:T(8,128)(2,1)S(1)}, s16[3,256,512]{2,1,0:T(8,128)(2,1)S(1)}, u32[]{:S(2)}, u32[]{:S(2)}) %collective-permute-start.23) | collective-permute-done | bytes 786464 | tf_op jit(solution)/shard_map/ppermute | solution.py:60
  154.7 4.3 %shard_map.62 = (f32[3,128,512]{2,1,0:T(8,128)S(1)}, s16[3,128,512]{2,1,0:T(8,128)(2,1)S(1)}, s16[3,128,512]{2,1,0:T(8,128)(2,1)S(1)}, s16[3,128,512]{2,1,0:T(8,128)(2,1)S(1)}) custom-call(s32[16]{0:T(128)S(1)} %dynamic-slice_bitcast_fusion.where_ref, f32[2,256,512]{2,1,0:T(8,128)S(1)} %copy-done.11, ...), custom_call_target="tpu_custom_call" | custom-call | flops 30000001024 | bytes 1000000 | tf_op jit(solution)/shard_map/pallas_call | solution.py:406
  159.0 4.0 %collective-permute-start.24 = (s16[3,128,512]{2,1,0:T(8,128)(2,1)S(1)}, s16[3,128,512]{2,1,0:T(8,128)(2,1)S(1)}, u32[]{:S(2)}, u32[]{:S(2)}) collective-permute-start(s16[3,128,512]{2,1,0:T(8,128)(2,1)S(1)} %get-tuple-element.60), channel_id=1, source_target_pairs={{0,8},{1,9},{2,10},{3,11},{4,12},{5,13},{6,14},{7,15},{8,0},{9,1},... | collective-permute-start | bytes 1179656 | tf_op jit(solution)/shard_map/ppermute | solution.py:60
  163.0 2.9 %collective-permute-start.25 = (s16[3,128,512]{2,1,0:T(8,128)(2,1)S(1)}, s16[3,128,512]{2,1,0:T(8,128)(2,1)S(1)}, u32[]{:S(2)}, u32[]{:S(2)}) collective-permute-start(s16[3,128,512]{2,1,0:T(8,128)(2,1)S(1)} %get-tuple-element.61), channel_id=1, source_target_pairs={{0,64},{1,65},{2,66},{3,67},{4,68},{5,69},{6,70},{7,71},{8,72},{9,... | collective-permute-start | bytes 1179656 | tf_op jit(solution)/shard_map/ppermute | solution.py:60
  165.9 0.3 collective-permute-start.26
  166.2 1.7 shard_map.58
  167.9 0.4 collective-permute-start.15
  168.3 2.9 %collective-permute-start.16 = (s16[1,128,512]{2,1,0:T(8,128)(2,1)S(1)}, s16[1,128,512]{2,1,0:T(8,128)(2,1)S(1)}, u32[]{:S(2)}, u32[]{:S(2)}) collective-permute-start(s16[1,128,512]{2,1,0:T(8,128)(2,1)S(1)} %get-tuple-element.48), channel_id=1, source_target_pairs={{0,64},{1,65},{2,66},{3,67},{4,68},{5,69},{6,70},{7,71},{8,72},{9,... | collective-permute-start | bytes 393224 | tf_op jit(solution)/shard_map/ppermute | solution.py:60
  171.2 0.5 collective-permute-start.17
  171.7 3.5 %collective-permute-done.25.y_ref = s16[3,128,512]{2,1,0:T(8,128)(2,1)S(1)} collective-permute-done((s16[3,128,512]{2,1,0:T(8,128)(2,1)S(1)}, s16[3,128,512]{2,1,0:T(8,128)(2,1)S(1)}, u32[]{:S(2)}, u32[]{:S(2)}) %collective-permute-start.25) | collective-permute-done | bytes 393248 | tf_op jit(solution)/shard_map/ppermute | solution.py:60
  175.2 9.1 %collective-permute-done.26.yc_ref = s16[3,128,512]{2,1,0:T(8,128)(2,1)S(1)} collective-permute-done((s16[3,128,512]{2,1,0:T(8,128)(2,1)S(1)}, s16[3,128,512]{2,1,0:T(8,128)(2,1)S(1)}, u32[]{:S(2)}, u32[]{:S(2)}) %collective-permute-start.26) | collective-permute-done | bytes 393248 | tf_op jit(solution)/shard_map/ppermute | solution.py:60
  184.3 3.9 %shard_map.63.rest_0_ = f32[4096,128]{1,0:T(8,128)} custom-call(s32[16]{0:T(128)S(1)} %dynamic-slice_bitcast_fusion.where_ref, f32[3,128,512]{2,1,0:T(8,128)S(1)} %get-tuple-element.59.keep_ref, s16[3,128,512]{2,1,0:T(8,128)(2,1)S(1)} %collective-permute-done.24.c_ref, s16[3,128,512]{2,1,0:T(8,128)(2,1)S(1)} %collective-permute-done.25.y_ref, ...), custom_call_target="tpu_custom_call" | custom-call | flops 30000001024 | bytes 1000000 | tf_op jit(solution)/shard_map/pallas_call | solution.py:446
  188.2 1.2 collective-permute-done.17.yc_ref
  189.4 4.3 %shard_map.64 = f32[4096,128]{1,0:T(8,128)} custom-call(s32[16]{0:T(128)S(1)} %dynamic-slice_bitcast_fusion.where_ref, f32[1,128,512]{2,1,0:T(8,128)S(1)} %get-tuple-element.46.keep_ref, s16[1,128,512]{2,1,0:T(8,128)(2,1)S(1)} %collective-permute-done.15.c_ref, ...), custom_call_target="tpu_custom_call", output_to_operand_aliasing={{}: (5, {})} | custom-call | flops 30000001024 | bytes 1000000 | tf_op jit(solution)/shard_map/pallas_call | solution.py:446
  (35 shorter events, 0.1 us)
Async XLA Ops:
  0.0 2.3 %copy-start = (s32[1152,1,1,1024]{3,2,1,0:T(1,128)S(1)}, s32[1152,1,1,1024]{3,2,1,0:T(1,128)}, u32[]{:S(2)}) copy-start(s32[1152,1,1,1024]{3,2,1,0:T(1,128)} %param.4) | copy-start | bytes 14155780
  2.3 0.7 copy-start.5
  3.0 0.7 copy-start.6
  4.6 8.0 %collective-permute-start = (f32[25,128]{1,0:T(8,128)S(1)}, f32[25,128]{1,0:T(8,128)S(1)}, u32[]{:S(2)}, u32[]{:S(2)}) collective-permute-start(f32[25,128]{1,0:T(8,128)S(1)} %shard_map.46.after_ref.part_ref.refs_1_), channel_id=1, source_target_pairs={{0,1},{1,0},{2,3},{3,2},{4,5},{5,4},{6,7},{7,6},{8,9},{9,8},{10,11... | collective-permute-start | bytes 38408 | tf_op jit(solution)/shard_map/ppermute | solution.py:60
  11.8 74.6 %collective-permute-start.5 = (s16[1152,1024]{1,0:T(8,128)(2,1)}, s16[1152,1024]{1,0:T(8,128)(2,1)}, u32[]{:S(2)}, u32[]{:S(2)}) collective-permute-start(s16[1152,1024]{1,0:T(8,128)(2,1)} %shard_map.47.after_ref.counts_ref.first_in.other_in), channel_id=1, source_target_pairs={{0,1},{1,0},{2,3},{3,2},{4,5},{5,4},{6,7},{7,6},{8,9},{9,8},{10,11... | collective-permute-start | bytes 7077896 | tf_op jit(solution)/shard_map/ppermute | solution.py:60
  12.6 0.6 copy-start.3
  13.2 8.3 %collective-permute-start.3 = (f32[25,128]{1,0:T(8,128)S(1)}, f32[25,128]{1,0:T(8,128)S(1)}, u32[]{:S(2)}, u32[]{:S(2)}) collective-permute-start(f32[25,128]{1,0:T(8,128)S(1)} %shard_map.48.after_ref), channel_id=1, source_target_pairs={{0,6},{1,7},{2,0},{3,1},{4,2},{5,3},{6,4},{7,5},{8,14},{9,15},{10,... | collective-permute-start | bytes 38408 | tf_op jit(solution)/shard_map/ppermute | solution.py:60
  15.8 8.3 %collective-permute-start.2 = (f32[25,128]{1,0:T(8,128)S(1)}, f32[25,128]{1,0:T(8,128)S(1)}, u32[]{:S(2)}, u32[]{:S(2)}) collective-permute-start(f32[25,128]{1,0:T(8,128)S(1)} %shard_map.48.after_ref), channel_id=1, source_target_pairs={{0,4},{1,5},{2,6},{3,7},{4,0},{5,1},{6,2},{7,3},{8,12},{9,13},{10,... | collective-permute-start | bytes 38408 | tf_op jit(solution)/shard_map/ppermute | solution.py:60
  16.3 7.8 %collective-permute-start.1 = (f32[25,128]{1,0:T(8,128)S(1)}, f32[25,128]{1,0:T(8,128)S(1)}, u32[]{:S(2)}, u32[]{:S(2)}) collective-permute-start(f32[25,128]{1,0:T(8,128)S(1)} %shard_map.48.after_ref), channel_id=1, source_target_pairs={{0,2},{1,3},{2,4},{3,5},{4,6},{5,7},{6,0},{7,1},{8,10},{9,11},{10,... | collective-permute-start | bytes 38408 | tf_op jit(solution)/shard_map/ppermute | solution.py:60
  19.9 26.8 %collective-permute-start.8 = (s16[1152,512]{1,0:T(8,128)(2,1)S(1)}, s16[1152,512]{1,0:T(8,128)(2,1)S(1)}, u32[]{:S(2)}, u32[]{:S(2)}) collective-permute-start(s16[1152,512]{1,0:T(8,128)(2,1)S(1)} %get-tuple-element.37), channel_id=1, source_target_pairs={{0,6},{1,7},{2,0},{3,1},{4,2},{5,3},{6,4},{7,5},{8,10},{9,11},{10,... | collective-permute-start | bytes 3538952 | tf_op jit(solution)/shard_map/ppermute | solution.py:60
  21.5 29.5 %collective-permute-start.9 = (s16[1152,512]{1,0:T(8,128)(2,1)S(1)}, s16[1152,512]{1,0:T(8,128)(2,1)S(1)}, u32[]{:S(2)}, u32[]{:S(2)}) collective-permute-start(s16[1152,512]{1,0:T(8,128)(2,1)S(1)} %get-tuple-element.38), channel_id=1, source_target_pairs={{0,10},{1,11},{2,12},{3,13},{4,14},{5,15},{6,8},{7,9},{8,6},{9,7},... | collective-permute-start | bytes 3538952 | tf_op jit(solution)/shard_map/ppermute | solution.py:60
  24.1 7.1 %collective-permute-start.10 = (f32[9,128]{1,0:T(8,128)S(1)}, f32[9,128]{1,0:T(8,128)S(1)}, u32[]{:S(2)}, u32[]{:S(2)}) collective-permute-start(f32[9,128]{1,0:T(8,128)S(1)} %slice_add_fusion.refs_0_.refs_2_.t_ref.refs_5_), channel_id=1, source_target_pairs={{0,8},{1,9},{2,10},{3,11},{4,12},{5,13},{6,14},{7,15},{8,0},{9,1},... | collective-permute-start | bytes 13832 | tf_op jit(solution)/shard_map/ppermute | solution.py:60
  29.8 27.0 %copy-start.1 = (bf16[1152,1024]{1,0:T(8,128)(2,1)}, bf16[1152,1024]{1,0:T(8,128)(2,1)S(1)}, u32[]{:S(2)}) copy-start(bf16[1152,1024]{1,0:T(8,128)(2,1)S(1)} %get-tuple-element.34.refs_0_.refs_2_) | copy-start | bytes 7077892
  29.8 42.1 %collective-permute-start.6 = (bf16[1152,512]{1,0:T(8,128)(2,1)S(1)}, bf16[1152,512]{1,0:T(8,128)(2,1)S(1)}, u32[]{:S(2)}, u32[]{:S(2)}) collective-permute-start(bf16[1152,512]{1,0:T(8,128)(2,1)S(1)} %get-tuple-element.35), channel_id=1, source_target_pairs={{0,6},{1,7},{2,0},{3,1},{4,2},{5,3},{6,4},{7,5},{8,10},{9,11},{10,... | collective-permute-start | bytes 3538952 | tf_op jit(solution)/shard_map/ppermute | solution.py:60
  31.2 45.1 %collective-permute-start.7 = (bf16[1152,512]{1,0:T(8,128)(2,1)S(1)}, bf16[1152,512]{1,0:T(8,128)(2,1)S(1)}, u32[]{:S(2)}, u32[]{:S(2)}) collective-permute-start(bf16[1152,512]{1,0:T(8,128)(2,1)S(1)} %get-tuple-element.36), channel_id=1, source_target_pairs={{0,10},{1,11},{2,12},{3,13},{4,14},{5,15},{6,8},{7,9},{8,6},{9,7},... | collective-permute-start | bytes 3538952 | tf_op jit(solution)/shard_map/ppermute | solution.py:60
  46.7 10.2 %collective-permute-start.4 = (bf16[1152,1024]{1,0:T(8,128)(2,1)S(1)}, bf16[1152,1024]{1,0:T(8,128)(2,1)}, u32[]{:S(2)}, u32[]{:S(2)}) collective-permute-start(bf16[1152,1024]{1,0:T(8,128)(2,1)S(1)} %get-tuple-element.34.refs_0_.refs_2_), channel_id=1, source_target_pairs={{0,8},{1,9},{2,10},{3,11},{4,12},{5,13},{6,14},{7,15},{8,0},{9,1},... | collective-permute-start | bytes 7077896 | tf_op jit(solution)/shard_map/ppermute | solution.py:60
  55.2 59.2 %collective-permute-start.12 = (bf16[2304,512]{1,0:T(8,128)(2,1)}, bf16[2304,512]{1,0:T(8,128)(2,1)}, u32[]{:S(2)}, u32[]{:S(2)}) collective-permute-start(bf16[2304,512]{1,0:T(8,128)(2,1)} %shard_map.51.refs_4_), channel_id=1, source_target_pairs={{0,6},{1,7},{2,0},{3,1},{4,2},{5,3},{6,4},{7,5},{8,10},{9,11},{10,... | collective-permute-start | bytes 7077896 | tf_op jit(solution)/shard_map/ppermute | solution.py:60
  66.3 16.3 %copy-start.7 = (f32[2,2,256,512]{3,2,1,0:T(8,128)}, f32[2,2,256,512]{3,2,1,0:T(8,128)S(1)}, u32[]{:S(2)}) copy-start(f32[2,2,256,512]{3,2,1,0:T(8,128)S(1)} %get-tuple-element.50.stay_ref) | copy-start | bytes 6291460
  66.3 20.2 %copy-start.4 = (f32[25,128]{1,0:T(8,128)S(1)}, f32[25,128]{1,0:T(8,128)}, u32[]{:S(2)}) copy-start(f32[25,128]{1,0:T(8,128)} %copy-done.3) | copy-start | bytes 38404
  66.3 27.9 %collective-permute-start.18 = (s16[2,2,256,512]{3,2,1,0:T(8,128)(2,1)S(1)}, s16[2,2,256,512]{3,2,1,0:T(8,128)(2,1)S(1)}, u32[]{:S(2)}, u32[]{:S(2)}) collective-permute-start(s16[2,2,256,512]{3,2,1,0:T(8,128)(2,1)S(1)} %get-tuple-element.39.refs_4_), channel_id=1, source_target_pairs={{0,16},{1,17},{2,18},{3,19},{4,20},{5,21},{6,22},{7,23},{8,56},{9,... | collective-permute-start | bytes 3145736 | tf_op jit(solution)/shard_map/ppermute | solution.py:60
  82.6 10.4 %collective-permute-start.20 = (s16[1,2,256,512]{3,2,1,0:T(8,128)(2,1)S(1)}, s16[1,2,256,512]{3,2,1,0:T(8,128)(2,1)S(1)}, u32[]{:S(2)}, u32[]{:S(2)}) collective-permute-start(s16[1,2,256,512]{3,2,1,0:T(8,128)(2,1)S(1)} %get-tuple-element.40.refs_2_.refs_7_), channel_id=1, source_target_pairs={{0,16},{1,17},{2,18},{3,19},{4,20},{5,21},{6,22},{7,23},{8,56},{9,... | collective-permute-start | bytes 1572872 | tf_op jit(solution)/shard_map/ppermute | solution.py:60
  91.3 2.8 %copy-start.2 = (bf16[1152,1024]{1,0:T(8,128)(2,1)}, bf16[1152,1024]{1,0:T(8,128)(2,1)S(1)}, u32[]{:S(2)}) copy-start(bf16[1152,1024]{1,0:T(8,128)(2,1)S(1)} %shard_map.54.refs_0_.refs_2_) | copy-start | bytes 7077892
  91.3 5.7 %collective-permute-start.11 = (bf16[1152,1024]{1,0:T(8,128)(2,1)S(1)}, bf16[1152,1024]{1,0:T(8,128)(2,1)}, u32[]{:S(2)}, u32[]{:S(2)}) collective-permute-start(bf16[1152,1024]{1,0:T(8,128)(2,1)S(1)} %shard_map.54.refs_0_.refs_2_), channel_id=1, source_target_pairs={{0,8},{1,9},{2,10},{3,11},{4,12},{5,13},{6,14},{7,15},{8,0},{9,1},... | collective-permute-start | bytes 7077896 | tf_op jit(solution)/shard_map/ppermute | solution.py:60
  93.0 1.7 copy-start.8
  94.1 51.8 %collective-permute-start.21 = (s16[1,256,512]{2,1,0:T(8,128)(2,1)}, s16[1,256,512]{2,1,0:T(8,128)(2,1)}, u32[]{:S(2)}, u32[]{:S(2)}) collective-permute-start(s16[1,256,512]{2,1,0:T(8,128)(2,1)} %get-tuple-element.55), channel_id=1, source_target_pairs={{0,48},{1,49},{2,50},{3,51},{4,52},{5,53},{6,54},{7,55},{8,24},{9,... | collective-permute-start | bytes 786440 | tf_op jit(solution)/shard_map/ppermute | solution.py:60
  96.0 15.4 %copy-start.10 = (f32[2,256,512]{2,1,0:T(8,128)}, f32[2,256,512]{2,1,0:T(8,128)S(1)}, u32[]{:S(2)}) copy-start(f32[2,256,512]{2,1,0:T(8,128)S(1)} %get-tuple-element.51.refs_0_) | copy-start | bytes 3145732
  96.0 50.0 %collective-permute-start.19 = (s16[2,256,512]{2,1,0:T(8,128)(2,1)S(1)}, s16[2,256,512]{2,1,0:T(8,128)(2,1)S(1)}, u32[]{:S(2)}, u32[]{:S(2)}) collective-permute-start(s16[2,256,512]{2,1,0:T(8,128)(2,1)S(1)} %get-tuple-element.52), channel_id=1, source_target_pairs={{0,48},{1,49},{2,50},{3,51},{4,52},{5,53},{6,54},{7,55},{8,24},{9,... | collective-permute-start | bytes 1572872 | tf_op jit(solution)/shard_map/ppermute | solution.py:60
  111.3 20.8 %collective-permute-start.22 = (s16[3,2,256,512]{3,2,1,0:T(8,128)(2,1)S(1)}, s16[3,2,256,512]{3,2,1,0:T(8,128)(2,1)S(1)}, u32[]{:S(2)}, u32[]{:S(2)}) collective-permute-start(s16[3,2,256,512]{3,2,1,0:T(8,128)(2,1)S(1)} %get-tuple-element.41.refs_5_), channel_id=1, source_target_pairs={{0,16},{1,17},{2,18},{3,19},{4,20},{5,21},{6,22},{7,23},{8,56},{9,... | collective-permute-start | bytes 4718600 | tf_op jit(solution)/shard_map/ppermute | solution.py:60
  124.6 18.7 %collective-permute-start.13 = (s16[2,2,256,512]{3,2,1,0:T(8,128)(2,1)S(1)}, s16[2,2,256,512]{3,2,1,0:T(8,128)(2,1)S(1)}, u32[]{:S(2)}, u32[]{:S(2)}) collective-permute-start(s16[2,2,256,512]{3,2,1,0:T(8,128)(2,1)S(1)} %get-tuple-element.43), channel_id=1, source_target_pairs={{0,16},{1,17},{2,18},{3,19},{4,20},{5,21},{6,22},{7,23},{8,56},{9,... | collective-permute-start | bytes 3145736 | tf_op jit(solution)/shard_map/ppermute | solution.py:60
  135.9 8.8 %copy-start.9 = (f32[3,256,512]{2,1,0:T(8,128)}, f32[3,256,512]{2,1,0:T(8,128)S(1)}, u32[]{:S(2)}) copy-start(f32[3,256,512]{2,1,0:T(8,128)S(1)} %get-tuple-element.57.refs_4_) | copy-start | bytes 4718596
  135.9 18.8 %collective-permute-start.23 = (s16[3,256,512]{2,1,0:T(8,128)(2,1)S(1)}, s16[3,256,512]{2,1,0:T(8,128)(2,1)S(1)}, u32[]{:S(2)}, u32[]{:S(2)}) collective-permute-start(s16[3,256,512]{2,1,0:T(8,128)(2,1)S(1)} %get-tuple-element.58), channel_id=1, source_target_pairs={{0,48},{1,49},{2,50},{3,51},{4,52},{5,53},{6,54},{7,55},{8,24},{9,... | collective-permute-start | bytes 2359304 | tf_op jit(solution)/shard_map/ppermute | solution.py:60
  143.3 11.3 %copy-start.11 = (f32[2,256,512]{2,1,0:T(8,128)S(1)}, f32[2,256,512]{2,1,0:T(8,128)}, u32[]{:S(2)}) copy-start(f32[2,256,512]{2,1,0:T(8,128)} %copy-done.10) | copy-start | bytes 3145732
  144.6 21.6 %collective-permute-start.14 = (s16[2,256,512]{2,1,0:T(8,128)(2,1)S(1)}, s16[2,256,512]{2,1,0:T(8,128)(2,1)S(1)}, u32[]{:S(2)}, u32[]{:S(2)}) collective-permute-start(s16[2,256,512]{2,1,0:T(8,128)(2,1)S(1)} %get-tuple-element.45), channel_id=1, source_target_pairs={{0,48},{1,49},{2,50},{3,51},{4,52},{5,53},{6,54},{7,55},{8,24},{9,... | collective-permute-start | bytes 1572872 | tf_op jit(solution)/shard_map/ppermute | solution.py:60
  159.0 12.2 %collective-permute-start.24 = (s16[3,128,512]{2,1,0:T(8,128)(2,1)S(1)}, s16[3,128,512]{2,1,0:T(8,128)(2,1)S(1)}, u32[]{:S(2)}, u32[]{:S(2)}) collective-permute-start(s16[3,128,512]{2,1,0:T(8,128)(2,1)S(1)} %get-tuple-element.60), channel_id=1, source_target_pairs={{0,8},{1,9},{2,10},{3,11},{4,12},{5,13},{6,14},{7,15},{8,0},{9,1},... | collective-permute-start | bytes 1179656 | tf_op jit(solution)/shard_map/ppermute | solution.py:60
  163.0 12.2 %collective-permute-start.25 = (s16[3,128,512]{2,1,0:T(8,128)(2,1)S(1)}, s16[3,128,512]{2,1,0:T(8,128)(2,1)S(1)}, u32[]{:S(2)}, u32[]{:S(2)}) collective-permute-start(s16[3,128,512]{2,1,0:T(8,128)(2,1)S(1)} %get-tuple-element.61), channel_id=1, source_target_pairs={{0,64},{1,65},{2,66},{3,67},{4,68},{5,69},{6,70},{7,71},{8,72},{9,... | collective-permute-start | bytes 1179656 | tf_op jit(solution)/shard_map/ppermute | solution.py:60
  165.9 18.3 %collective-permute-start.26 = (s16[3,128,512]{2,1,0:T(8,128)(2,1)S(1)}, s16[3,128,512]{2,1,0:T(8,128)(2,1)S(1)}, u32[]{:S(2)}, u32[]{:S(2)}) collective-permute-start(s16[3,128,512]{2,1,0:T(8,128)(2,1)S(1)} %get-tuple-element.62), channel_id=1, source_target_pairs={{0,72},{1,73},{2,74},{3,75},{4,76},{5,77},{6,78},{7,79},{8,64},{9,... | collective-permute-start | bytes 1179656 | tf_op jit(solution)/shard_map/ppermute | solution.py:60
  167.9 20.2 %collective-permute-start.15 = (s16[1,128,512]{2,1,0:T(8,128)(2,1)S(1)}, s16[1,128,512]{2,1,0:T(8,128)(2,1)S(1)}, u32[]{:S(2)}, u32[]{:S(2)}) collective-permute-start(s16[1,128,512]{2,1,0:T(8,128)(2,1)S(1)} %get-tuple-element.47), channel_id=1, source_target_pairs={{0,8},{1,9},{2,10},{3,11},{4,12},{5,13},{6,14},{7,15},{8,0},{9,1},... | collective-permute-start | bytes 393224 | tf_op jit(solution)/shard_map/ppermute | solution.py:60
  168.3 19.9 %collective-permute-start.16 = (s16[1,128,512]{2,1,0:T(8,128)(2,1)S(1)}, s16[1,128,512]{2,1,0:T(8,128)(2,1)S(1)}, u32[]{:S(2)}, u32[]{:S(2)}) collective-permute-start(s16[1,128,512]{2,1,0:T(8,128)(2,1)S(1)} %get-tuple-element.48), channel_id=1, source_target_pairs={{0,64},{1,65},{2,66},{3,67},{4,68},{5,69},{6,70},{7,71},{8,72},{9,... | collective-permute-start | bytes 393224 | tf_op jit(solution)/shard_map/ppermute | solution.py:60
  171.2 18.2 %collective-permute-start.17 = (s16[1,128,512]{2,1,0:T(8,128)(2,1)S(1)}, s16[1,128,512]{2,1,0:T(8,128)(2,1)S(1)}, u32[]{:S(2)}, u32[]{:S(2)}) collective-permute-start(s16[1,128,512]{2,1,0:T(8,128)(2,1)S(1)} %get-tuple-element.49), channel_id=1, source_target_pairs={{0,72},{1,73},{2,74},{3,75},{4,76},{5,77},{6,78},{7,79},{8,64},{9,... | collective-permute-start | bytes 393224 | tf_op jit(solution)/shard_map/ppermute | solution.py:60
